TPU v7x, 256 devices: a whole 4x4x8 slice. The times are simulated.
256 devices in a mesh: prompt: 16 (over z, core), sample: 16 (over x, y).
Axes of the slice: x: 4, y: 4, z: 8, core: 2. Of those that a mesh axis runs over, the one named last changes fastest.
Arguments:
- prompt_latent: bfloat16 [16, 73728], P('prompt', 'sample'), may hold values from -8 to 8
- resp_latent: bfloat16 [16, 1179648], P('prompt', 'sample'), may hold values from -6 to 6
- queries: bfloat16 [16, 2048, 12288], P('prompt', 'sample'), may hold values from -300 to 300
- d_attended: bfloat16 [16, 2048, 8192], P('prompt', 'sample'), may hold values from -6 to 6
- w_kv: bfloat16 [512, 16384], P(None, 'prompt'), may hold values from -0.25 to 0.25
- seg_ids: int32 [16, 2048], P('prompt', 'sample'), may hold values from 0 to 8, as said below
- live: int32 [16, 16], P('prompt', 'sample'), may hold values from 32 to 128, as said below
Outputs:
- attended: bfloat16 [16, 2048, 8192], P('prompt', 'sample')
- d_queries: bfloat16 [16, 2048, 12288], P('prompt', 'sample')
- d_prompt_latent: bfloat16 [16, 73728], P('prompt', 'sample')
- d_resp_latent: bfloat16 [16, 1179648], P('prompt', 'sample')
Inputs may be any that keep to these rules, and one draw needn't show every extreme that they name: `seg_ids`: nondecreasing along each device's 128 slots, 0 at its first slot, rising by one at each of exactly 8 response starts; equal values mark one response. In every group some device has all 128 slots live.
All inputs are finite; a program needn't handle non-finite values.
Results may differ from a plain program's by a relative error of at most 0.02.
Values may be sent and summed in bfloat16 or wider, within the bound.
No kernel may reach another device: no remote copies, remote signals or barrier semaphores. Data moves between devices by JAX's collectives and lax.ppermute only.
A program may use at most 192 MiB of HBM per device.

v0:
```python
import functools
import jax
import jax.numpy as jnp
from jax import lax
from jax.experimental import pallas as pl
from jax.experimental.pallas import tpu as pltpu
from jax.sharding import PartitionSpec as P

DC = 512
DR = 64
DL = 576
DN = 128
DQ = 192
ROWS = 128
KEYS = 256
HEADS = 4
SCALE = 1.0 / DQ**0.5
LOG2E = 1.4426950408889634
F32 = jnp.float32
BF16 = jnp.bfloat16


def mm(a, b, ca, cb):
    return lax.dot_general(a, b, (((ca,), (cb,)), ((), ())), preferred_element_type=F32)


def attend_kernel(order_ref, lat_ref, rope_ref, bias_ref, alive_ref, w_ref, q_ref, g_ref, acc_in,
                  *rest):
    out_ref, dq_ref, acc_ref, kv_ref, dkv_ref = rest[-5:]

    @pl.when(pl.program_id(0) == 0)
    def _():
        acc_ref[...] = acc_in[...]

    w = w_ref[...].reshape(DC, HEADS * 256)
    kv_ref[...] = mm(lat_ref[...], w, 1, 0).astype(BF16)
    rope_even = rope_ref[:, :128]
    rope_odd = rope_ref[:, 128:]
    bias = bias_ref[...]
    alive = alive_ref[...]
    low = lax.broadcasted_iota(jnp.int32, (KEYS, 128), 1) < DR
    for pair in range(HEADS // 2):
        merged = None
        for odd in range(2):
            head = pair * 2 + odd
            at = pair * 384 + odd * 128
            q = q_ref[:, at : at + 256]
            g = g_ref[:, head * 128 : (head + 1) * 128]
            key = kv_ref[:, head * 256 : head * 256 + 128]
            value = kv_ref[:, head * 256 + 128 : (head + 1) * 256]
            if odd:
                turned = jnp.concatenate([key[:, DR:], key[:, :DR]], axis=1)
                zero = jnp.zeros_like(turned)
                key_row = jnp.concatenate(
                    [jnp.where(low, zero, turned), jnp.where(low, turned, rope_odd)], axis=1
                )
            else:
                key_row = jnp.concatenate([key, rope_even], axis=1)
            s = mm(key_row, q, 1, 1)
            s = jnp.concatenate([s[:ROWS], s[ROWS:] + bias], axis=0)
            top = jnp.max(s, axis=0, keepdims=True)
            e = jnp.exp2((s - top) * (SCALE * LOG2E))
            inv = alive / jnp.sum(e, axis=0, keepdims=True)
            a_b = (e * inv).astype(BF16)
            d_a = mm(value, g, 1, 1)
            delta = jnp.sum(e * d_a, axis=0, keepdims=True) * inv
            d_s = ((e * (d_a - delta)) * (inv * SCALE)).astype(BF16)
            out_ref[:, head * 128 : (head + 1) * 128] = mm(a_b, value, 0, 0).astype(BF16)
            d_q = mm(d_s, key_row, 0, 0)
            if odd:
                dq_ref[:, pair * 384 : pair * 384 + 128] = merged[:, :128].astype(BF16)
                dq_ref[:, pair * 384 + 128 : pair * 384 + 256] = (
                    merged[:, 128:] + d_q[:, :128]
                ).astype(BF16)
                dq_ref[:, pair * 384 + 256 : pair * 384 + 384] = d_q[:, 128:].astype(BF16)
            else:
                merged = d_q
            d_k = mm(d_s, q, 1, 0)
            d_v = mm(a_b, g, 1, 0)
            if odd:
                d_key = jnp.concatenate([d_k[:, DR:128], d_k[:, 128 : 128 + DR]], axis=1)
                acc_ref[:, DC + 128 :] += d_k[:, 128:]
            else:
                d_key = d_k[:, :128]
                acc_ref[:, DC : DC + 128] += d_k[:, 128:]
            dkv_ref[:, head * 256 : head * 256 + 128] = d_key.astype(BF16)
            dkv_ref[:, head * 256 + 128 : (head + 1) * 256] = d_v.astype(BF16)
    acc_ref[:, :DC] += mm(dkv_ref[...], w, 1, 1)


def attend(order, lat, rope, bias, alive, w, queries, grads, acc, carried):
    steps = order.shape[0]
    fixed = lambda i, order: (0, 0)
    split = lambda i, order: (0, order[i])
    in_specs = [
        pl.BlockSpec((KEYS, DC), fixed),
        pl.BlockSpec((KEYS, 256), fixed),
        pl.BlockSpec((ROWS, ROWS), fixed),
        pl.BlockSpec((1, ROWS), fixed),
        pl.BlockSpec((1, DC, 1024), lambda i, order: (order[i], 0, 0)),
        pl.BlockSpec((ROWS, 768), split),
        pl.BlockSpec((ROWS, 512), split),
        pl.BlockSpec((KEYS, 768), fixed),
    ]
    args = [order, lat, rope, bias, alive, w, queries, grads, acc]
    aliases = {8: 2}
    if carried is not None:
        in_specs += [pl.BlockSpec(memory_space=pl.ANY)] * 2
        args += list(carried)
        aliases.update({9: 0, 10: 1})
    return pl.pallas_call(
        attend_kernel,
        grid_spec=pltpu.PrefetchScalarGridSpec(
            num_scalar_prefetch=1,
            grid=(steps,),
            in_specs=in_specs,
            out_specs=[
                pl.BlockSpec((ROWS, 512), split),
                pl.BlockSpec((ROWS, 768), split),
                pl.BlockSpec((KEYS, 768), fixed),
            ],
            scratch_shapes=[
                pltpu.VMEM((KEYS, 1024), BF16),
                pltpu.VMEM((KEYS, 1024), BF16),
            ],
        ),
        out_shape=[
            jax.ShapeDtypeStruct((ROWS, 8192), BF16),
            jax.ShapeDtypeStruct((ROWS, 12288), BF16),
            jax.ShapeDtypeStruct((KEYS, 768), F32),
        ],
        input_output_aliases=aliases,
        compiler_params=pltpu.CompilerParams(vmem_limit_bytes=40 * 1024 * 1024),
        cost_estimate=pl.CostEstimate(
            flops=steps * 800_000_000, bytes_accessed=steps * 1_800_000, transcendentals=steps * 131072
        ),
    )(*args)


def body(prompt_latent, resp_latent, queries, d_attended, w_kv, seg_ids, live):
    w = lax.all_gather(w_kv, "prompt", axis=0)
    whole_prompt = lax.all_gather(prompt_latent, "sample", axis=1, tiled=True).reshape(-1, DL)
    rows = jnp.concatenate([whole_prompt, resp_latent.reshape(-1, DL)], axis=0)
    rope = rows[:, DC:]
    blank = jnp.zeros_like(rope)
    rope = jnp.concatenate([rope, blank, blank, rope], axis=1)
    seg = seg_ids[0]
    position = jnp.arange(ROWS, dtype=jnp.int32)
    seen = (
        (seg[:, None] == seg[None, :])
        & (position[:, None] <= position[None, :])
        & (position[:, None] < live[0, 0])
    )
    bias = jnp.where(seen, F32(0.0), F32(-1e30))
    alive = (position < live[0, 0]).astype(F32)[None, :]
    order = jnp.arange(16, dtype=jnp.int32)
    attended, d_queries, acc = attend(
        order, rows[:, :DC], rope, bias, alive, w, queries[0], d_attended[0],
        jnp.zeros((KEYS, 768), F32), None,
    )
    d_rope = acc[:, DC : DC + DR] + acc[:, DC + 128 + DR :]
    term = jnp.concatenate([acc[:, :DC], d_rope], axis=1).astype(BF16)
    pieces = lax.all_to_all(term[:ROWS].reshape(16, -1), "sample", 0, 0)
    d_prompt = jnp.sum(pieces.astype(F32), axis=0).astype(BF16).reshape(1, -1)
    d_resp = term[ROWS:].reshape(1, -1)
    return (attended[None], d_queries[None], d_prompt, d_resp)


def solution(mesh):
    rows = P("prompt", "sample")
    wide = P("prompt", "sample", None)
    return jax.shard_map(
        body,
        mesh=mesh,
        in_specs=(rows, rows, wide, wide, P(None, "prompt"), rows, rows),
        out_specs=(wide, wide, rows, rows),
        check_vma=False,
    )
```

profile of v0, /device:TPU:1, one launch (start us, length us, event | category | flops | bytes accessed | tf_op | source)
XLA Modules:
  0.0 176.5 jit_solution(12920091414278366792)
XLA Ops:
  7.2 0.7 all-gather.3.cloned.1.call-update
  7.9 19.8 %all_gather.9 = bf16[1,73728]{1,0:T(2,128)(2,1)S(1)} all-gather(bf16[1,4608]{1,0:T(2,128)(2,1)} %param.7), channel_id=1, replica_groups=mesh['prompt'=16,'sample'=16] {'sample'}, dimensions={1}, use_global_device_ids=true | all-gather | bytes 156672 | tf_op jit(solution)/shard_map/all_gather | solution.py:142
  27.7 0.9 reduce.2
  28.6 0.2 reshape.40
  28.8 1.8 %reduce.3 = bf16[73728]{0:T(1024)(128)(2,1)S(1)} reduce(bf16[1,73728]{1,0:T(2,128)(2,1)} %param.8, bf16[]{:T(256)} %constant.14), dimensions={0}, to_apply=%param.8.reduce_sub_computation | reduce | bytes 294914 | tf_op args[1]
  30.5 0.2 reshape.41
  31.4 0.1 pad.3.clone
  31.5 0.1 fusion.3.bias_ref
  31.6 0.1 pad_maximum_fusion.1.rope_ref
  31.7 77.8 %all-gather.3.cloned.1.call-done = bf16[8192,1024]{1,0:T(8,128)(2,1)} async-done(((bf16[512,1024]{1,0:T(8,128)(2,1)}), bf16[8192,1024]{1,0:T(8,128)(2,1)}) %all-gather.3.cloned.1.call-update) | async-done | bytes 16777232 | tf_op jit(solution)/shard_map/all_gather | solution.py:141
  109.5 0.1 broadcast_in_dim.23.acc_in
  109.6 1.9 %copy-done = bf16[1,128,12288]{2,1,0:T(8,128)(2,1)S(1)} copy-done((bf16[1,128,12288]{2,1,0:T(8,128)(2,1)S(1)}, bf16[1,128,12288]{2,1,0:T(8,128)(2,1)}, u32[]{:S(2)}) %copy-start) | copy-done | bytes 3145752
  111.5 40.8 %shard_map.102 = (bf16[128,8192]{1,0:T(8,128)(2,1)}, bf16[128,12288]{1,0:T(8,128)(2,1)}, f32[256,768]{1,0:T(8,128)S(1)}) custom-call(s32[16]{0:T(128)S(1)} %iota.16.order_ref, bf16[256,512]{1,0:T(8,128)(2,1)S(1)} %slice.29.lat_ref, bf16[256,256]{1,0:T(8,128)(2,1)S(1)} %pad_maximum_fusion.1.rope_ref, ...), custom_call_target="tpu_custom_call", output_to_operand_aliasing={{2}: (8, {})} | custom-call | flops 12800000000 | bytes 28800000 | tf_op jit(solution)/shard_map/pallas_call | solution.py:111
  152.3 0.1 add_convert_fusion
  152.4 0.2 all_to_all.8
  152.6 0.5 broadcast.16
  153.2 1.5 reduce.4
  154.6 0.7 reshape.47
  155.3 6.5 %all-to-all-start = ((bf16[16,2,2304]{2,1,0:T(2,128)(2,1)}), bf16[16,2,2304]{2,1,0:T(2,128)(2,1)S(1)}, u32[]{:S(2)}, u32[]{:S(2)}) async-start(bf16[16,2,2304]{2,1,0:T(2,128)(2,1)} %reshape.47), calls=%async_computation | async-start | bytes 294912 | tf_op jit(solution)/shard_map/all_to_all | solution.py:163
  161.9 0.9 reshape.43
  162.8 5.8 %all-to-all-done = bf16[16,2,2304]{2,1,0:T(2,128)(2,1)S(1)} async-done(((bf16[16,2,2304]{2,1,0:T(2,128)(2,1)}), bf16[16,2,2304]{2,1,0:T(2,128)(2,1)S(1)}, u32[]{:S(2)}, u32[]{:S(2)}) %all-to-all-start) | async-done | bytes 147488 | tf_op jit(solution)/shard_map/all_to_all | solution.py:163
  168.6 0.1 reshape.48
  168.7 0.3 reduce_sum.12
  169.0 0.6 reshape.42
  (16 shorter events, 0.2 us)
Async XLA Ops:
  7.2 24.4 %copy-start.2 = (s32[1,128]{1,0:T(1,128)S(1)}, s32[1,128]{1,0:T(1,128)}, u32[]{:S(2)}) copy-start(s32[1,128]{1,0:T(1,128)} %param.12) | copy-start | bytes 1540
  7.2 102.4 %copy-start.1 = (bf16[1,128,8192]{2,1,0:T(8,128)(2,1)S(1)}, bf16[1,128,8192]{2,1,0:T(8,128)(2,1)}, u32[]{:S(2)}) copy-start(bf16[1,128,8192]{2,1,0:T(8,128)(2,1)} %param.10) | copy-start | bytes 6291460
  7.2 102.3 %all-gather.3.cloned.1.call-start = ((), (), s32[]{:S(2)}) async-start(), calls=%async_computation.1 | async-start | bytes 17825792 | tf_op jit(solution)/shard_map/all_gather | solution.py:141
  109.6 1.9 %copy-start = (bf16[1,128,12288]{2,1,0:T(8,128)(2,1)S(1)}, bf16[1,128,12288]{2,1,0:T(8,128)(2,1)}, u32[]{:S(2)}) copy-start(bf16[1,128,12288]{2,1,0:T(8,128)(2,1)} %param.9) | copy-start | bytes 9437188
  155.3 13.3 %all-to-all-start = ((bf16[16,2,2304]{2,1,0:T(2,128)(2,1)}), bf16[16,2,2304]{2,1,0:T(2,128)(2,1)S(1)}, u32[]{:S(2)}, u32[]{:S(2)}) async-start(bf16[16,2,2304]{2,1,0:T(2,128)(2,1)} %reshape.47), calls=%async_computation | async-start | bytes 294912 | tf_op jit(solution)/shard_map/all_to_all | solution.py:163
Sparse Core Ops, SparseCore 0:
  9.8 99.6 all-gather.2
where the time goes:
time: 177 us; the launch traced here: 176 us
  waiting for transfers between devices  84.3 us (48%)
  Pallas kernels  40.8 us (23%)
  blocking collectives  19.8 us (11%)
  between operations  14.8 us (8%)
  starting transfers between devices  6.57 us (4%)
  local copies, waits for them, and re-layouts  5.52 us (3%)
  other arithmetic  4.72 us (3%)
    all_gather x1, waiting for transfers between devices, body(): w = lax.all_gather(w_kv, 'prompt', axis=0)  77.8 us
    pallas_call x1, Pallas kernels, attend(): pl.pallas_call(attend_kernel, grid_spec=pltpu.PrefetchScalarGridSpec(num_...  40.8 us
    all_gather x1, blocking collectives, body(): lax.all_gather(prompt_latent, 'sample', axis=1, tiled=True).reshape(-1, DL)  19.8 us
    all_to_all x1, starting transfers between devices, body(): pieces = lax.all_to_all(term[:ROWS].reshape(16, -1), 'sample', 0, 0)  6.53 us
    all_to_all x1, waiting for transfers between devices, body(): pieces = lax.all_to_all(term[:ROWS].reshape(16, -1), 'sample', 0, 0)  5.81 us
  transfers between devices with their start and end apart: 2, of which 2 were waited for; matrix products, arithmetic and copies ran while one was open for 2% of the time, Pallas kernels for 0%

commit v1 on v0

--- a/solution.py
+++ b/solution.py
@@ -14,6 +14,7 @@
 ROWS = 128
 KEYS = 256
 HEADS = 4
+FLOPS = 4_000_000_000
 SCALE = 1.0 / DQ**0.5
 LOG2E = 1.4426950408889634
 F32 = jnp.float32
@@ -24,23 +25,39 @@
     return lax.dot_general(a, b, (((ca,), (cb,)), ((), ())), preferred_element_type=F32)
 
 
-def attend_kernel(order_ref, lat_ref, rope_ref, bias_ref, alive_ref, w_ref, q_ref, g_ref, acc_in,
+def attend_kernel(parts, order_ref, lat_ref, rope_ref, bias_ref, alive_ref, q_ref, g_ref, acc_in,
                   *rest):
-    out_ref, dq_ref, acc_ref, kv_ref, dkv_ref = rest[-5:]
+    w_refs = rest[:parts]
+    out_ref, dq_ref, acc_ref, kv_ref, dkv_ref, w_scratch = rest[-6:]
 
     @pl.when(pl.program_id(0) == 0)
     def _():
         acc_ref[...] = acc_in[...]
 
-    w = w_ref[...].reshape(DC, HEADS * 256)
+    if parts == 1:
+        w_ref = w_refs[0].at[0]
+    else:
+        w_ref = w_scratch
+        for index, ref in enumerate(w_refs):
+            quarter, late = index // 5 * 4 + min(index % 5, 3), index % 5 == 4
+            rows = pl.ds(quarter * 64, 64)
+            if index % 5 < 3:
+                w_scratch[rows, :] = ref[0]
+            else:
+
+                @pl.when((pl.program_id(0) >= pl.num_programs(0) // 2) == late)
+                def _():
+                    w_scratch[rows, :] = ref[0]
+
+    w = w_ref[...]
     kv_ref[...] = mm(lat_ref[...], w, 1, 0).astype(BF16)
     rope_even = rope_ref[:, :128]
     rope_odd = rope_ref[:, 128:]
     bias = bias_ref[...]
     alive = alive_ref[...]
     low = lax.broadcasted_iota(jnp.int32, (KEYS, 128), 1) < DR
+    staged = []
     for pair in range(HEADS // 2):
-        merged = None
         for odd in range(2):
             head = pair * 2 + odd
             at = pair * 384 + odd * 128
@@ -58,11 +75,17 @@
                 key_row = jnp.concatenate([key, rope_even], axis=1)
             s = mm(key_row, q, 1, 1)
             s = jnp.concatenate([s[:ROWS], s[ROWS:] + bias], axis=0)
+            d_a = mm(value, g, 1, 1)
+            staged.append((q, g, value, key_row, s, d_a))
+    for pair in range(HEADS // 2):
+        merged = None
+        for odd in range(2):
+            head = pair * 2 + odd
+            q, g, value, key_row, s, d_a = staged[head]
             top = jnp.max(s, axis=0, keepdims=True)
             e = jnp.exp2((s - top) * (SCALE * LOG2E))
             inv = alive / jnp.sum(e, axis=0, keepdims=True)
             a_b = (e * inv).astype(BF16)
-            d_a = mm(value, g, 1, 1)
             delta = jnp.sum(e * d_a, axis=0, keepdims=True) * inv
             d_s = ((e * (d_a - delta)) * (inv * SCALE)).astype(BF16)
             out_ref[:, head * 128 : (head + 1) * 128] = mm(a_b, value, 0, 0).astype(BF16)
@@ -88,7 +111,7 @@
     acc_ref[:, :DC] += mm(dkv_ref[...], w, 1, 1)
 
 
-def attend(order, lat, rope, bias, alive, w, queries, grads, acc, carried):
+def attend(order, lat, rope, bias, alive, weights, queries, grads, acc, carried):
     steps = order.shape[0]
     fixed = lambda i, order: (0, 0)
     split = lambda i, order: (0, order[i])
@@ -97,19 +120,28 @@
         pl.BlockSpec((KEYS, 256), fixed),
         pl.BlockSpec((ROWS, ROWS), fixed),
         pl.BlockSpec((1, ROWS), fixed),
-        pl.BlockSpec((1, DC, 1024), lambda i, order: (order[i], 0, 0)),
         pl.BlockSpec((ROWS, 768), split),
         pl.BlockSpec((ROWS, 512), split),
         pl.BlockSpec((KEYS, 768), fixed),
     ]
-    args = [order, lat, rope, bias, alive, w, queries, grads, acc]
-    aliases = {8: 2}
+    args = [order, lat, rope, bias, alive, queries, grads, acc]
+    half = steps // 2
+    for index, w in enumerate(weights):
+        if index % 5 < 3:
+            place = lambda i, order: (i, 0, 0)
+        elif index % 5 == 3:
+            place = lambda i, order: (jnp.minimum(i, half - 1), 0, 0)
+        else:
+            place = lambda i, order: (jnp.maximum(i - half, 0), 0, 0)
+        in_specs.append(pl.BlockSpec((1,) + w.shape[1:], place))
+        args.append(w)
+    aliases = {7: 2}
     if carried is not None:
+        aliases.update({len(args): 0, len(args) + 1: 1})
         in_specs += [pl.BlockSpec(memory_space=pl.ANY)] * 2
         args += list(carried)
-        aliases.update({9: 0, 10: 1})
     return pl.pallas_call(
-        attend_kernel,
+        functools.partial(attend_kernel, len(weights)),
         grid_spec=pltpu.PrefetchScalarGridSpec(
             num_scalar_prefetch=1,
             grid=(steps,),
@@ -122,6 +154,7 @@
             scratch_shapes=[
                 pltpu.VMEM((KEYS, 1024), BF16),
                 pltpu.VMEM((KEYS, 1024), BF16),
+                pltpu.VMEM((DC, 1024), BF16),
             ],
         ),
         out_shape=[
@@ -132,14 +165,81 @@
         input_output_aliases=aliases,
         compiler_params=pltpu.CompilerParams(vmem_limit_bytes=40 * 1024 * 1024),
         cost_estimate=pl.CostEstimate(
-            flops=steps * 800_000_000, bytes_accessed=steps * 1_800_000, transcendentals=steps * 131072
+            flops=steps * FLOPS, bytes_accessed=steps * 1_800_000, transcendentals=0
         ),
     )(*args)
 
 
+def at(x, y, z, core):
+    return ((z % 8) * 2 + core) * 16 + (x % 4) * 4 + y % 4
+
+
+CHIPS = [(x, y, z) for x in range(4) for y in range(4) for z in range(8)]
+SWAP = [(at(x, y, z, c), at(x, y, z, 1 - c)) for x, y, z in CHIPS for c in range(2)]
+
+
+def along_z(step):
+    return [(at(x, y, z, c), at(x, y, z + step, c)) for x, y, z in CHIPS for c in range(2)]
+
+
+def along_plane(step):
+    return [(at(x, y, z, 0), at(x + step, y, z, 0)) for x, y, z in CHIPS] + [
+        (at(x, y, z, 1), at(x, y + step, z, 1)) for x, y, z in CHIPS
+    ]
+
+
+def send(a, pairs):
+    return lax.ppermute(a, ("prompt", "sample"), pairs)
+
+
+def places():
+    prompt, sample = lax.axis_index("prompt"), lax.axis_index("sample")
+    z, core = prompt // 2, prompt % 2
+    x, y = sample // 4, sample % 4
+    mine = jnp.where(core == 0, x, y)
+    other = jnp.where(core == 0, y, x)
+    return z, core, mine, other
+
+
+def z_slices(w):
+    z, core, mine, other = places()
+    parts = w.reshape(8, -1, w.shape[1])
+    keep = lax.dynamic_index_in_dim(parts, core * 4 + mine, 0, keepdims=True)
+    give = lax.dynamic_index_in_dim(parts, (1 - core) * 4 + other, 0, keepdims=True)
+    got = send(give, SWAP)
+    here = jnp.where(core == 0, jnp.concatenate([keep, got]), jnp.concatenate([got, keep]))
+    down, up = [here], [here]
+    for _ in range(3):
+        down.append(send(down[-1], along_z(1)))
+        up.append(send(up[-1], along_z(-1)))
+    far = jnp.concatenate([send(down[3][:1], along_z(1)), send(up[3][1:], along_z(-1))])
+    return down, up, far
+
+
+def plane_gather(group):
+    half = group.shape[0] // 2
+    left = send(group, along_plane(1))
+    right = send(group, along_plane(-1))
+    early = send(left[:half], along_plane(1))
+    late = send(right[half:], along_plane(-1))
+    pieces = [group, left, right, early, late]
+    return pieces + [send(piece, SWAP) for piece in pieces]
+
+
+def row_order():
+    z, core, mine, other = places()
+    turn = jnp.array([0, 3, 1, 2], jnp.int32)
+    return jnp.concatenate([core * 4 + (mine + turn) % 4, (1 - core) * 4 + (other + turn) % 4])
+
+
 def body(prompt_latent, resp_latent, queries, d_attended, w_kv, seg_ids, live):
-    w = lax.all_gather(w_kv, "prompt", axis=0)
-    whole_prompt = lax.all_gather(prompt_latent, "sample", axis=1, tiled=True).reshape(-1, DL)
+    z, core, mine, other = places()
+    prompt = 2 * z + core
+    down, up, far = z_slices(w_kv)
+    pair = jnp.stack([w_kv, send(w_kv, SWAP)])
+    whole_prompt = lax.all_to_all(
+        jnp.tile(prompt_latent.reshape(-1, DL), (16, 1)), "sample", 0, 0, tiled=True
+    )
     rows = jnp.concatenate([whole_prompt, resp_latent.reshape(-1, DL)], axis=0)
     rope = rows[:, DC:]
     blank = jnp.zeros_like(rope)
@@ -153,14 +253,34 @@
     )
     bias = jnp.where(seen, F32(0.0), F32(-1e30))
     alive = (position < live[0, 0]).astype(F32)[None, :]
-    order = jnp.arange(16, dtype=jnp.int32)
+    lat = rows[:, :DC]
+    index = jnp.arange(DC, dtype=jnp.int32)
+    source = jnp.repeat(row_order() * 64, 64) + index % 64
+    turn = (index[:, None] == source[None, :]).astype(BF16)
+    lat_turned = jnp.dot(lat, turn, preferred_element_type=F32).astype(BF16)
+
     attended, d_queries, acc = attend(
-        order, rows[:, :DC], rope, bias, alive, w, queries[0], d_attended[0],
+        jnp.stack([prompt, prompt ^ 1]), lat, rope, bias, alive, [pair], queries[0], d_attended[0],
         jnp.zeros((KEYS, 768), F32), None,
     )
-    d_rope = acc[:, DC : DC + DR] + acc[:, DC + 128 + DR :]
-    term = jnp.concatenate([acc[:, :DC], d_rope], axis=1).astype(BF16)
-    pieces = lax.all_to_all(term[:ROWS].reshape(16, -1), "sample", 0, 0)
+    first = acc
+    acc = jnp.zeros((KEYS, 768), F32)
+    for group, steps in enumerate(((-1, 1, -2, 2), (-3, 3, 4))):
+        pieces = []
+        for step in steps:
+            pieces.append(far if step == 4 else (up[step] if step > 0 else down[-step]))
+        weights = plane_gather(jnp.concatenate(pieces))
+        order = jnp.concatenate([2 * ((z + step) % 8) + jnp.arange(2) for step in steps])
+        attended, d_queries, acc = attend(
+            order.astype(jnp.int32), lat_turned, rope, bias, alive,
+            weights, queries[0], d_attended[0], acc, (attended, d_queries),
+        )
+    latent = first[:, :DC] + jnp.dot(
+        acc[:, :DC], turn.T.astype(F32), precision=lax.Precision.HIGHEST, preferred_element_type=F32
+    )
+    both = first[:, DC:] + acc[:, DC:]
+    term = jnp.concatenate([latent, both[:, :DR] + both[:, 128 + DR :]], axis=1).astype(BF16)
+    pieces = lax.all_to_all(term[:ROWS], "sample", 0, 0, tiled=True).reshape(16, -1, DL)
     d_prompt = jnp.sum(pieces.astype(F32), axis=0).astype(BF16).reshape(1, -1)
     d_resp = term[ROWS:].reshape(1, -1)
     return (attended[None], d_queries[None], d_prompt, d_resp)

time: 177 us -> 127 us (0.72)
  waiting for transfers between devices: 84.3 us -> 26.7 us
  starting transfers between devices: 6.57 us -> 48 us
  blocking collectives: 19.8 us -> 0 us
  between operations: 14.8 us -> 1.63 us
  Pallas kernels: 40.8 us -> 32.2 us
  local copies, waits for them, and re-layouts: 5.52 us -> 11 us
    all_gather x1 -> x0, waiting for transfers between devices: 77.8 us -> none  [body(): w = lax.all_gather(w_kv, 'prompt', axis=0)]
    ppermute x0 -> x28, starting transfers between devices: none -> 34.8 us  [send(): return lax.ppermute(a, ('prompt', 'sample'), pairs)]
    ppermute x0 -> x28, waiting for transfers between devices: none -> 20.8 us  [send(): return lax.ppermute(a, ('prompt', 'sample'), pairs)]
    all_gather x1 -> x0, blocking collectives: 19.8 us -> none  [body(): lax.all_gather(prompt_latent, 'sample', axis=1, tiled=True).reshape(-1, DL)]
    pallas_call x1 -> x3, Pallas kernels: 40.8 us -> 32.2 us  [attend(): pl.pallas_call(functools.partial(attend_kernel, len(weights)), grid_spec=...]
    all_to_all x1 -> x2, starting transfers between devices: 6.53 us -> 13.1 us  [the longest x1 7.58 us: body(): lax.all_to_all(jnp.tile(prompt_latent.reshape(-1, DL), (16, 1)), 'sample'...]
    unnamed x9 -> x16, local copies, waits for them, and re-layouts: 2.71 us -> 4.32 us
    all_to_all x1 -> x2, waiting for transfers between devices: 5.81 us -> 5.86 us  [the longest x1 5.86 us: body(): lax.all_to_all(term[:ROWS], 'sample', 0, 0, tiled=True).reshape(16, -1, DL)]
  transfers between devices with their start and end apart: 2 -> 30, of which waited for: 2 -> 7; matrix products, arithmetic and copies ran while one was open for 2% -> 11% of each run, Pallas kernels for 0% -> 16%
where the time goes in v1:
time: 127 us
  starting transfers between devices  48 us (38%)
  Pallas kernels  32.2 us (25%)
  waiting for transfers between devices  26.7 us (21%)
  local copies, waits for them, and re-layouts  11 us (9%)
  other arithmetic  6.22 us (5%)
  between operations  1.63 us (1%)
    ppermute x28, starting transfers between devices, send(): return lax.ppermute(a, ('prompt', 'sample'), pairs)  34.8 us
    pallas_call x3, Pallas kernels, attend(): pl.pallas_call(functools.partial(attend_kernel, len(weights)), grid_spec=...  32.2 us
    ppermute x28, waiting for transfers between devices, send(): return lax.ppermute(a, ('prompt', 'sample'), pairs)  20.8 us
    all_to_all x1, starting transfers between devices, body(): lax.all_to_all(jnp.tile(prompt_latent.reshape(-1, DL), (16, 1)), 'sample'...  7.58 us
    all_to_all x1, waiting for transfers between devices, body(): lax.all_to_all(term[:ROWS], 'sample', 0, 0, tiled=True).reshape(16, -1, DL)  5.86 us
    all_to_all x1, starting transfers between devices, body(): lax.all_to_all(term[:ROWS], 'sample', 0, 0, tiled=True).reshape(16, -1, DL)  5.55 us
    unnamed x16, local copies, waits for them, and re-layouts  4.32 us
    unnamed x2, other arithmetic  2.56 us
  transfers between devices with their start and end apart: 30, of which 7 were waited for; matrix products, arithmetic and copies ran while one was open for 11% of the time, Pallas kernels for 16%

profile of v1, /device:TPU:1, one launch (start us, length us, event | category | flops | bytes accessed | tf_op | source)
XLA Modules:
  0.0 126.8 jit_solution(13055050200692862008)
XLA Ops:
  2.2 7.6 %all-to-all-start = ((bf16[16,8,576]{2,1,0:T(8,128)(2,1)}), bf16[16,8,576]{2,1,0:T(8,128)(2,1)S(1)}, u32[]{:S(2)}, u32[]{:S(2)}) async-start(bf16[16,8,576]{2,1,0:T(8,128)(2,1)} %tile.9), calls=%async_computation | async-start | bytes 327680 | tf_op jit(solution)/shard_map/all_to_all | solution.py:240
  13.3 1.7 %collective-permute-start.1 = (bf16[2,64,1024]{2,1,0:T(8,128)(2,1)S(1)}, bf16[2,64,1024]{2,1,0:T(8,128)(2,1)S(1)}, u32[]{:S(2)}, u32[]{:S(2)}) collective-permute-start(bf16[2,64,1024]{2,1,0:T(8,128)(2,1)S(1)} %maximum_select_fusion), channel_id=1, source_target_pairs={{0,32},{16,48},{32,64},{48,80},{64,96},{80,112},{96,128},{112,144}... | collective-permute-start | bytes 786440 | tf_op jit(solution)/shard_map/ppermute | solution.py:192
  15.7 4.0 %collective-permute-start.2 = (bf16[2,64,1024]{2,1,0:T(8,128)(2,1)S(1)}, bf16[2,64,1024]{2,1,0:T(8,128)(2,1)S(1)}, u32[]{:S(2)}, u32[]{:S(2)}) collective-permute-start(bf16[2,64,1024]{2,1,0:T(8,128)(2,1)S(1)} %maximum_select_fusion), channel_id=1, source_target_pairs={{0,224},{16,240},{32,0},{48,16},{64,32},{80,48},{96,64},{112,80},{... | collective-permute-start | bytes 786440 | tf_op jit(solution)/shard_map/ppermute | solution.py:192
  19.7 5.6 %collective-permute-done.1 = bf16[2,64,1024]{2,1,0:T(8,128)(2,1)S(1)} collective-permute-done((bf16[2,64,1024]{2,1,0:T(8,128)(2,1)S(1)}, bf16[2,64,1024]{2,1,0:T(8,128)(2,1)S(1)}, u32[]{:S(2)}, u32[]{:S(2)}) %collective-permute-start.1) | collective-permute-done | bytes 262176 | tf_op jit(solution)/shard_map/ppermute | solution.py:192
  25.4 3.1 %collective-permute-start.4 = (bf16[2,64,1024]{2,1,0:T(8,128)(2,1)S(1)}, bf16[2,64,1024]{2,1,0:T(8,128)(2,1)S(1)}, u32[]{:S(2)}, u32[]{:S(2)}) collective-permute-start(bf16[2,64,1024]{2,1,0:T(8,128)(2,1)S(1)} %collective-permute-done.2), channel_id=1, source_target_pairs={{0,224},{16,240},{32,0},{48,16},{64,32},{80,48},{96,64},{112,80},{... | collective-permute-start | bytes 786440 | tf_op jit(solution)/shard_map/ppermute | solution.py:192
  29.9 3.6 %collective-permute-done.3 = bf16[2,64,1024]{2,1,0:T(8,128)(2,1)S(1)} collective-permute-done((bf16[2,64,1024]{2,1,0:T(8,128)(2,1)S(1)}, bf16[2,64,1024]{2,1,0:T(8,128)(2,1)S(1)}, u32[]{:S(2)}, u32[]{:S(2)}) %collective-permute-start.3) | collective-permute-done | bytes 262176 | tf_op jit(solution)/shard_map/ppermute | solution.py:192
  34.9 1.6 %collective-permute-start.5 = (bf16[8,64,1024]{2,1,0:T(8,128)(2,1)}, bf16[8,64,1024]{2,1,0:T(8,128)(2,1)S(1)}, u32[]{:S(2)}, u32[]{:S(2)}) collective-permute-start(bf16[8,64,1024]{2,1,0:T(8,128)(2,1)} %constant_dynamic-update-slice_fusion.rest_0_), channel_id=1, source_target_pairs={{0,4},{32,36},{64,68},{96,100},{128,132},{160,164},{192,196},{224,... | collective-permute-start | bytes 3145736 | tf_op jit(solution)/shard_map/ppermute | solution.py:192
  36.5 2.7 %collective-permute-start.16 = (bf16[2,64,1024]{2,1,0:T(8,128)(2,1)S(1)}, bf16[2,64,1024]{2,1,0:T(8,128)(2,1)S(1)}, u32[]{:S(2)}, u32[]{:S(2)}) collective-permute-start(bf16[2,64,1024]{2,1,0:T(8,128)(2,1)S(1)} %collective-permute-done.4), channel_id=1, source_target_pairs={{0,224},{16,240},{32,0},{48,16},{64,32},{80,48},{96,64},{112,80},{... | collective-permute-start | bytes 786440 | tf_op jit(solution)/shard_map/ppermute | solution.py:192
  40.6 2.8 %collective-permute-done.15 = bf16[2,64,1024]{2,1,0:T(8,128)(2,1)S(1)} collective-permute-done((bf16[2,64,1024]{2,1,0:T(8,128)(2,1)S(1)}, bf16[2,64,1024]{2,1,0:T(8,128)(2,1)S(1)}, u32[]{:S(2)}, u32[]{:S(2)}) %collective-permute-start.15) | collective-permute-done | bytes 262176 | tf_op jit(solution)/shard_map/ppermute | solution.py:192
  43.6 2.7 %collective-permute-start.18 = (bf16[1,64,1024]{2,1,0:T(8,128)(2,1)S(1)}, bf16[1,64,1024]{2,1,0:T(8,128)(2,1)S(1)}, u32[]{:S(2)}, u32[]{:S(2)}) collective-permute-start(bf16[1,64,1024]{2,1,0:T(8,128)(2,1)S(1)} %slice.69), channel_id=1, source_target_pairs={{0,224},{16,240},{32,0},{48,16},{64,32},{80,48},{96,64},{112,80},{... | collective-permute-start | bytes 393224 | tf_op jit(solution)/shard_map/ppermute | solution.py:192
  48.9 3.8 %collective-permute-start.9 = (bf16[8,64,1024]{2,1,0:T(8,128)(2,1)}, bf16[8,64,1024]{2,1,0:T(8,128)(2,1)}, u32[]{:S(2)}, u32[]{:S(2)}) collective-permute-start(bf16[8,64,1024]{2,1,0:T(8,128)(2,1)} %constant_dynamic-update-slice_fusion.rest_0_), channel_id=1, source_target_pairs={{0,16},{16,0},{32,48},{48,32},{64,80},{80,64},{96,112},{112,96},{1... | collective-permute-start | bytes 3145736 | tf_op jit(solution)/shard_map/ppermute | solution.py:192
  55.3 1.8 %collective-permute-start.20 = (bf16[6,64,1024]{2,1,0:T(8,128)(2,1)}, bf16[6,64,1024]{2,1,0:T(8,128)(2,1)}, u32[]{:S(2)}, u32[]{:S(2)}) collective-permute-start(bf16[6,64,1024]{2,1,0:T(8,128)(2,1)} %constant_dynamic-update-slice_fusion.4.rest_0_), channel_id=1, source_target_pairs={{0,12},{32,44},{64,76},{96,108},{128,140},{160,172},{192,204},{224... | collective-permute-start | bytes 2359304 | tf_op jit(solution)/shard_map/ppermute | solution.py:192
  57.2 1.8 %reduce.3 = bf16[73728]{0:T(1024)(128)(2,1)S(1)} reduce(bf16[1,73728]{1,0:T(2,128)(2,1)} %param.9, bf16[]{:T(256)} %constant.151), dimensions={0}, to_apply=%param.9.reduce_sub_computation | reduce | bytes 294914 | tf_op args[1]
  59.6 7.0 %collective-permute-done.19.rest_1_ = bf16[6,64,1024]{2,1,0:T(8,128)(2,1)S(1)} collective-permute-done((bf16[6,64,1024]{2,1,0:T(8,128)(2,1)}, bf16[6,64,1024]{2,1,0:T(8,128)(2,1)S(1)}, u32[]{:S(2)}, u32[]{:S(2)}) %collective-permute-start.19) | collective-permute-done | bytes 786464 | tf_op jit(solution)/shard_map/ppermute | solution.py:192
  68.6 1.5 %collective-permute-start.10 = (bf16[8,64,1024]{2,1,0:T(8,128)(2,1)S(1)}, bf16[8,64,1024]{2,1,0:T(8,128)(2,1)S(1)}, u32[]{:S(2)}, u32[]{:S(2)}) collective-permute-start(bf16[8,64,1024]{2,1,0:T(8,128)(2,1)S(1)} %collective-permute-done.5.rest_1_), channel_id=1, source_target_pairs={{0,16},{16,0},{32,48},{48,32},{64,80},{80,64},{96,112},{112,96},{1... | collective-permute-start | bytes 3145736 | tf_op jit(solution)/shard_map/ppermute | solution.py:192
  70.3 1.6 %pad_maximum_fusion.rest_0_ = bf16[2,512,1024]{2,1,0:T(8,128)(2,1)S(1)} fusion(bf16[1,512,1024]{2,1,0:T(8,128)(2,1)} %bitcast.9, bf16[1,512,1024]{2,1,0:T(8,128)(2,1)S(1)} %bitcast.24), kind=kLoop, calls=%fused_computation | loop fusion | flops 1048576 | bytes 4194304 | tf_op jit(solution)/shard_map/stack | solution.py:239
  71.9 1.3 %slice.71 = bf16[3,64,1024]{2,1,0:T(8,128)(2,1)S(1)} slice(bf16[6,64,1024]{2,1,0:T(8,128)(2,1)} %collective-permute-done.20.rest_2_), slice={[3:6], [0:64], [0:1024]} | slice | bytes 786432 | tf_op jit(solution)/shard_map/slice | solution.py:224
  73.2 2.2 %collective-permute-start.22 = (bf16[3,64,1024]{2,1,0:T(8,128)(2,1)S(1)}, bf16[3,64,1024]{2,1,0:T(8,128)(2,1)S(1)}, u32[]{:S(2)}, u32[]{:S(2)}) collective-permute-start(bf16[3,64,1024]{2,1,0:T(8,128)(2,1)S(1)} %slice.71), channel_id=1, source_target_pairs={{0,12},{32,44},{64,76},{96,108},{128,140},{160,172},{192,204},{224... | collective-permute-start | bytes 1179656 | tf_op jit(solution)/shard_map/ppermute | solution.py:192
  76.6 1.8 %collective-permute-start.13 = (bf16[4,64,1024]{2,1,0:T(8,128)(2,1)S(1)}, bf16[4,64,1024]{2,1,0:T(8,128)(2,1)S(1)}, u32[]{:S(2)}, u32[]{:S(2)}) collective-permute-start(bf16[4,64,1024]{2,1,0:T(8,128)(2,1)S(1)} %collective-permute-done.8.rest_4_), channel_id=1, source_target_pairs={{0,16},{16,0},{32,48},{48,32},{64,80},{80,64},{96,112},{112,96},{1... | collective-permute-start | bytes 1572872 | tf_op jit(solution)/shard_map/ppermute | solution.py:192
  78.5 4.2 %shard_map.111 = (bf16[128,8192]{1,0:T(8,128)(2,1)}, bf16[128,12288]{1,0:T(8,128)(2,1)}, f32[256,768]{1,0:T(8,128)S(1)}) custom-call(s32[2]{0:T(128)S(1)} %pad_add_fusion.2.order_ref, bf16[256,512]{1,0:T(8,128)(2,1)S(1)} %fusion.4.lat_ref, bf16[256,256]{1,0:T(8,128)(2,1)S(1)} %pad_maximum_fusion.2.rope_ref, ...), custom_call_target="tpu_custom_call", output_to_operand_aliasing={{2}: (7, {})} | custom-call | flops 8000000000 | bytes 3600000 | tf_op jit(solution)/shard_map/pallas_call | solution.py:143
  84.1 15.8 %shard_map.112 = (bf16[128,8192]{1,0:T(8,128)(2,1)}, bf16[128,12288]{1,0:T(8,128)(2,1)}, f32[256,768]{1,0:T(8,128)S(1)}) custom-call(s32[8]{0:T(128)S(1)} %pad_add_fusion.1.order_ref, bf16[256,512]{1,0:T(8,128)(2,1)S(1)} %convolution_convert_fusion.lat_ref, ...), custom_call_target="tpu_custom_call", output_to_operand_aliasing={{2}: (7, {}), {0}: (18, {}), {1}: (19, {})} | custom-call | flops 32000000000 | bytes 14400000 | tf_op jit(solution)/shard_map/pallas_call | solution.py:143
  100.0 12.1 %shard_map.113 = (bf16[128,8192]{1,0:T(8,128)(2,1)}, bf16[128,12288]{1,0:T(8,128)(2,1)}, f32[256,768]{1,0:T(8,128)S(1)}) custom-call(s32[6]{0:T(128)S(1)} %pad_add_fusion.order_ref, bf16[256,512]{1,0:T(8,128)(2,1)S(1)} %convolution_convert_fusion.lat_ref, ...), custom_call_target="tpu_custom_call", output_to_operand_aliasing={{2}: (7, {}), {0}: (18, {}), {1}: (19, {})} | custom-call | flops 24000000000 | bytes 10800000 | tf_op jit(solution)/shard_map/pallas_call | solution.py:143
  113.7 5.6 %all-to-all-start.1 = ((bf16[16,8,576]{2,1,0:T(8,128)(2,1)}), bf16[16,8,576]{2,1,0:T(8,128)(2,1)S(1)}, u32[]{:S(2)}, u32[]{:S(2)}) async-start(bf16[16,8,576]{2,1,0:T(8,128)(2,1)} %get-tuple-element.25), calls=%async_computation.1 | async-start | bytes 327680 | tf_op jit(solution)/shard_map/all_to_all | solution.py:283
  120.2 5.9 %all-to-all-done.1 = bf16[16,8,576]{2,1,0:T(8,128)(2,1)S(1)} async-done(((bf16[16,8,576]{2,1,0:T(8,128)(2,1)}), bf16[16,8,576]{2,1,0:T(8,128)(2,1)S(1)}, u32[]{:S(2)}, u32[]{:S(2)}) %all-to-all-start.1) | async-done | bytes 147488 | tf_op jit(solution)/shard_map/all_to_all | solution.py:283
  (101 shorter events, 23.4 us)
Async XLA Ops:
  2.2 57.2 %all-to-all-start = ((bf16[16,8,576]{2,1,0:T(8,128)(2,1)}), bf16[16,8,576]{2,1,0:T(8,128)(2,1)S(1)}, u32[]{:S(2)}, u32[]{:S(2)}) async-start(bf16[16,8,576]{2,1,0:T(8,128)(2,1)} %tile.9), calls=%async_computation | async-start | bytes 327680 | tf_op jit(solution)/shard_map/all_to_all | solution.py:240
  9.8 58.2 %collective-permute-start.14 = (bf16[512,1024]{1,0:T(8,128)(2,1)}, bf16[512,1024]{1,0:T(8,128)(2,1)}, u32[]{:S(2)}, u32[]{:S(2)}) collective-permute-start(bf16[512,1024]{1,0:T(8,128)(2,1)} %param.12), channel_id=1, source_target_pairs={{0,16},{16,0},{32,48},{48,32},{64,80},{80,64},{96,112},{112,96},{1... | collective-permute-start | bytes 3145736 | tf_op jit(solution)/shard_map/ppermute | solution.py:192
  13.3 12.0 %collective-permute-start.1 = (bf16[2,64,1024]{2,1,0:T(8,128)(2,1)S(1)}, bf16[2,64,1024]{2,1,0:T(8,128)(2,1)S(1)}, u32[]{:S(2)}, u32[]{:S(2)}) collective-permute-start(bf16[2,64,1024]{2,1,0:T(8,128)(2,1)S(1)} %maximum_select_fusion), channel_id=1, source_target_pairs={{0,32},{16,48},{32,64},{48,80},{64,96},{80,112},{96,128},{112,144}... | collective-permute-start | bytes 786440 | tf_op jit(solution)/shard_map/ppermute | solution.py:192
  15.7 9.7 %collective-permute-start.2 = (bf16[2,64,1024]{2,1,0:T(8,128)(2,1)S(1)}, bf16[2,64,1024]{2,1,0:T(8,128)(2,1)S(1)}, u32[]{:S(2)}, u32[]{:S(2)}) collective-permute-start(bf16[2,64,1024]{2,1,0:T(8,128)(2,1)S(1)} %maximum_select_fusion), channel_id=1, source_target_pairs={{0,224},{16,240},{32,0},{48,16},{64,32},{80,48},{96,64},{112,80},{... | collective-permute-start | bytes 786440 | tf_op jit(solution)/shard_map/ppermute | solution.py:192
  25.4 8.1 %collective-permute-start.3 = (bf16[2,64,1024]{2,1,0:T(8,128)(2,1)S(1)}, bf16[2,64,1024]{2,1,0:T(8,128)(2,1)S(1)}, u32[]{:S(2)}, u32[]{:S(2)}) collective-permute-start(bf16[2,64,1024]{2,1,0:T(8,128)(2,1)S(1)} %collective-permute-done.1), channel_id=1, source_target_pairs={{0,32},{16,48},{32,64},{48,80},{64,96},{80,112},{96,128},{112,144}... | collective-permute-start | bytes 786440 | tf_op jit(solution)/shard_map/ppermute | solution.py:192
  25.4 8.8 %collective-permute-start.4 = (bf16[2,64,1024]{2,1,0:T(8,128)(2,1)S(1)}, bf16[2,64,1024]{2,1,0:T(8,128)(2,1)S(1)}, u32[]{:S(2)}, u32[]{:S(2)}) collective-permute-start(bf16[2,64,1024]{2,1,0:T(8,128)(2,1)S(1)} %collective-permute-done.2), channel_id=1, source_target_pairs={{0,224},{16,240},{32,0},{48,16},{64,32},{80,48},{96,64},{112,80},{... | collective-permute-start | bytes 786440 | tf_op jit(solution)/shard_map/ppermute | solution.py:192
  34.9 20.4 %collective-permute-start.5 = (bf16[8,64,1024]{2,1,0:T(8,128)(2,1)}, bf16[8,64,1024]{2,1,0:T(8,128)(2,1)S(1)}, u32[]{:S(2)}, u32[]{:S(2)}) collective-permute-start(bf16[8,64,1024]{2,1,0:T(8,128)(2,1)} %constant_dynamic-update-slice_fusion.rest_0_), channel_id=1, source_target_pairs={{0,4},{32,36},{64,68},{96,100},{128,132},{160,164},{192,196},{224,... | collective-permute-start | bytes 3145736 | tf_op jit(solution)/shard_map/ppermute | solution.py:192
  39.4 20.0 %collective-permute-start.6 = (bf16[8,64,1024]{2,1,0:T(8,128)(2,1)}, bf16[8,64,1024]{2,1,0:T(8,128)(2,1)S(1)}, u32[]{:S(2)}, u32[]{:S(2)}) collective-permute-start(bf16[8,64,1024]{2,1,0:T(8,128)(2,1)} %constant_dynamic-update-slice_fusion.rest_0_), channel_id=1, source_target_pairs={{0,12},{32,44},{64,76},{96,108},{128,140},{160,172},{192,204},{224... | collective-permute-start | bytes 3145736 | tf_op jit(solution)/shard_map/ppermute | solution.py:192
  43.6 9.8 %collective-permute-start.18 = (bf16[1,64,1024]{2,1,0:T(8,128)(2,1)S(1)}, bf16[1,64,1024]{2,1,0:T(8,128)(2,1)S(1)}, u32[]{:S(2)}, u32[]{:S(2)}) collective-permute-start(bf16[1,64,1024]{2,1,0:T(8,128)(2,1)S(1)} %slice.69), channel_id=1, source_target_pairs={{0,224},{16,240},{32,0},{48,16},{64,32},{80,48},{96,64},{112,80},{... | collective-permute-start | bytes 393224 | tf_op jit(solution)/shard_map/ppermute | solution.py:192
  48.9 19.7 %collective-permute-start.9 = (bf16[8,64,1024]{2,1,0:T(8,128)(2,1)}, bf16[8,64,1024]{2,1,0:T(8,128)(2,1)}, u32[]{:S(2)}, u32[]{:S(2)}) collective-permute-start(bf16[8,64,1024]{2,1,0:T(8,128)(2,1)} %constant_dynamic-update-slice_fusion.rest_0_), channel_id=1, source_target_pairs={{0,16},{16,0},{32,48},{48,32},{64,80},{80,64},{96,112},{112,96},{1... | collective-permute-start | bytes 3145736 | tf_op jit(solution)/shard_map/ppermute | solution.py:192
  54.0 12.6 %collective-permute-start.19 = (bf16[6,64,1024]{2,1,0:T(8,128)(2,1)}, bf16[6,64,1024]{2,1,0:T(8,128)(2,1)S(1)}, u32[]{:S(2)}, u32[]{:S(2)}) collective-permute-start(bf16[6,64,1024]{2,1,0:T(8,128)(2,1)} %constant_dynamic-update-slice_fusion.4.rest_0_), channel_id=1, source_target_pairs={{0,4},{32,36},{64,68},{96,100},{128,132},{160,164},{192,196},{224,... | collective-permute-start | bytes 2359304 | tf_op jit(solution)/shard_map/ppermute | solution.py:192
  55.3 14.8 %collective-permute-start.20 = (bf16[6,64,1024]{2,1,0:T(8,128)(2,1)}, bf16[6,64,1024]{2,1,0:T(8,128)(2,1)}, u32[]{:S(2)}, u32[]{:S(2)}) collective-permute-start(bf16[6,64,1024]{2,1,0:T(8,128)(2,1)} %constant_dynamic-update-slice_fusion.4.rest_0_), channel_id=1, source_target_pairs={{0,12},{32,44},{64,76},{96,108},{128,140},{160,172},{192,204},{224... | collective-permute-start | bytes 2359304 | tf_op jit(solution)/shard_map/ppermute | solution.py:192
  59.4 13.8 %collective-permute-start.7 = (bf16[4,64,1024]{2,1,0:T(8,128)(2,1)S(1)}, bf16[4,64,1024]{2,1,0:T(8,128)(2,1)S(1)}, u32[]{:S(2)}, u32[]{:S(2)}) collective-permute-start(bf16[4,64,1024]{2,1,0:T(8,128)(2,1)S(1)} %slice.66), channel_id=1, source_target_pairs={{0,4},{32,36},{64,68},{96,100},{128,132},{160,164},{192,196},{224,... | collective-permute-start | bytes 1572872 | tf_op jit(solution)/shard_map/ppermute | solution.py:192
  66.6 8.8 %collective-permute-start.8 = (bf16[4,64,1024]{2,1,0:T(8,128)(2,1)S(1)}, bf16[4,64,1024]{2,1,0:T(8,128)(2,1)S(1)}, u32[]{:S(2)}, u32[]{:S(2)}) collective-permute-start(bf16[4,64,1024]{2,1,0:T(8,128)(2,1)S(1)} %slice.67), channel_id=1, source_target_pairs={{0,12},{32,44},{64,76},{96,108},{128,140},{160,172},{192,204},{224... | collective-permute-start | bytes 1572872 | tf_op jit(solution)/shard_map/ppermute | solution.py:192
  68.0 8.6 %collective-permute-start.21 = (bf16[3,64,1024]{2,1,0:T(8,128)(2,1)S(1)}, bf16[3,64,1024]{2,1,0:T(8,128)(2,1)S(1)}, u32[]{:S(2)}, u32[]{:S(2)}) collective-permute-start(bf16[3,64,1024]{2,1,0:T(8,128)(2,1)S(1)} %slice.70), channel_id=1, source_target_pairs={{0,4},{32,36},{64,68},{96,100},{128,132},{160,164},{192,196},{224,... | collective-permute-start | bytes 1179656 | tf_op jit(solution)/shard_map/ppermute | solution.py:192
  68.6 14.7 %collective-permute-start.10 = (bf16[8,64,1024]{2,1,0:T(8,128)(2,1)S(1)}, bf16[8,64,1024]{2,1,0:T(8,128)(2,1)S(1)}, u32[]{:S(2)}, u32[]{:S(2)}) collective-permute-start(bf16[8,64,1024]{2,1,0:T(8,128)(2,1)S(1)} %collective-permute-done.5.rest_1_), channel_id=1, source_target_pairs={{0,16},{16,0},{32,48},{48,32},{64,80},{80,64},{96,112},{112,96},{1... | collective-permute-start | bytes 3145736 | tf_op jit(solution)/shard_map/ppermute | solution.py:192
  70.1 13.7 %collective-permute-start.11 = (bf16[8,64,1024]{2,1,0:T(8,128)(2,1)S(1)}, bf16[8,64,1024]{2,1,0:T(8,128)(2,1)S(1)}, u32[]{:S(2)}, u32[]{:S(2)}) collective-permute-start(bf16[8,64,1024]{2,1,0:T(8,128)(2,1)S(1)} %collective-permute-done.6.rest_2_), channel_id=1, source_target_pairs={{0,16},{16,0},{32,48},{48,32},{64,80},{80,64},{96,112},{112,96},{1... | collective-permute-start | bytes 3145736 | tf_op jit(solution)/shard_map/ppermute | solution.py:192
  73.2 9.5 %collective-permute-start.22 = (bf16[3,64,1024]{2,1,0:T(8,128)(2,1)S(1)}, bf16[3,64,1024]{2,1,0:T(8,128)(2,1)S(1)}, u32[]{:S(2)}, u32[]{:S(2)}) collective-permute-start(bf16[3,64,1024]{2,1,0:T(8,128)(2,1)S(1)} %slice.71), channel_id=1, source_target_pairs={{0,12},{32,44},{64,76},{96,108},{128,140},{160,172},{192,204},{224... | collective-permute-start | bytes 1179656 | tf_op jit(solution)/shard_map/ppermute | solution.py:192
  82.7 17.2 %collective-permute-start.23 = (bf16[6,64,1024]{2,1,0:T(8,128)(2,1)}, bf16[6,64,1024]{2,1,0:T(8,128)(2,1)S(1)}, u32[]{:S(2)}, u32[]{:S(2)}) collective-permute-start(bf16[6,64,1024]{2,1,0:T(8,128)(2,1)} %constant_dynamic-update-slice_fusion.4.rest_0_), channel_id=1, source_target_pairs={{0,16},{16,0},{32,48},{48,32},{64,80},{80,64},{96,112},{112,96},{1... | collective-permute-start | bytes 2359304 | tf_op jit(solution)/shard_map/ppermute | solution.py:192
  82.7 17.3 %collective-permute-start.24 = (bf16[6,64,1024]{2,1,0:T(8,128)(2,1)S(1)}, bf16[6,64,1024]{2,1,0:T(8,128)(2,1)S(1)}, u32[]{:S(2)}, u32[]{:S(2)}) collective-permute-start(bf16[6,64,1024]{2,1,0:T(8,128)(2,1)S(1)} %collective-permute-done.19.rest_1_), channel_id=1, source_target_pairs={{0,16},{16,0},{32,48},{48,32},{64,80},{80,64},{96,112},{112,96},{1... | collective-permute-start | bytes 2359304 | tf_op jit(solution)/shard_map/ppermute | solution.py:192
  83.2 16.8 %collective-permute-start.25 = (bf16[6,64,1024]{2,1,0:T(8,128)(2,1)}, bf16[6,64,1024]{2,1,0:T(8,128)(2,1)S(1)}, u32[]{:S(2)}, u32[]{:S(2)}) collective-permute-start(bf16[6,64,1024]{2,1,0:T(8,128)(2,1)} %collective-permute-done.20.rest_2_), channel_id=1, source_target_pairs={{0,16},{16,0},{32,48},{48,32},{64,80},{80,64},{96,112},{112,96},{1... | collective-permute-start | bytes 2359304 | tf_op jit(solution)/shard_map/ppermute | solution.py:192
  83.3 16.6 %collective-permute-start.26 = (bf16[3,64,1024]{2,1,0:T(8,128)(2,1)S(1)}, bf16[3,64,1024]{2,1,0:T(8,128)(2,1)S(1)}, u32[]{:S(2)}, u32[]{:S(2)}) collective-permute-start(bf16[3,64,1024]{2,1,0:T(8,128)(2,1)S(1)} %collective-permute-done.21.rest_3_), channel_id=1, source_target_pairs={{0,16},{16,0},{32,48},{48,32},{64,80},{80,64},{96,112},{112,96},{1... | collective-permute-start | bytes 1179656 | tf_op jit(solution)/shard_map/ppermute | solution.py:192
  83.8 16.2 %collective-permute-start.27 = (bf16[3,64,1024]{2,1,0:T(8,128)(2,1)S(1)}, bf16[3,64,1024]{2,1,0:T(8,128)(2,1)S(1)}, u32[]{:S(2)}, u32[]{:S(2)}) collective-permute-start(bf16[3,64,1024]{2,1,0:T(8,128)(2,1)S(1)} %collective-permute-done.22.rest_4_), channel_id=1, source_target_pairs={{0,16},{16,0},{32,48},{48,32},{64,80},{80,64},{96,112},{112,96},{1... | collective-permute-start | bytes 1179656 | tf_op jit(solution)/shard_map/ppermute | solution.py:192
  113.7 12.4 %all-to-all-start.1 = ((bf16[16,8,576]{2,1,0:T(8,128)(2,1)}), bf16[16,8,576]{2,1,0:T(8,128)(2,1)S(1)}, u32[]{:S(2)}, u32[]{:S(2)}) async-start(bf16[16,8,576]{2,1,0:T(8,128)(2,1)} %get-tuple-element.25), calls=%async_computation.1 | async-start | bytes 327680 | tf_op jit(solution)/shard_map/all_to_all | solution.py:283
  (11 other events, 107.8 us)

commit v2 on v0

v2 whole, which is shorter than its diff:
```python
import functools
import jax
import jax.numpy as jnp
from jax import lax
from jax.experimental import pallas as pl
from jax.experimental.pallas import tpu as pltpu
from jax.sharding import PartitionSpec as P

DC = 512
DR = 64
DL = 576
DN = 128
DQ = 192
ROWS = 128
KEYS = 256
HEADS = 4
VMEM = 60
FLOPS = 4_000_000_000
SCALE = 1.0 / DQ**0.5
LOG2E = 1.4426950408889634
F32 = jnp.float32
BF16 = jnp.bfloat16


def mm(a, b, ca, cb):
    return lax.dot_general(a, b, (((ca,), (cb,)), ((), ())), preferred_element_type=F32)


def attend_kernel(layout, more, last, order_ref, rows_hbm, mask_hbm, q_hbm, g_hbm, *rest):
    w_hbm = rest[more : more + 1 + max(entry[0] for entry in layout)]
    outs = rest[:-11][-4 if last else -3 :]
    out_ref, dq_ref = outs[:2]
    rows_ref, mask_ref, q_all, g_all, w_all, before_ref, acc_ref, kv_ref, dkv_ref = rest[-11:-2]
    arrived, loaded = rest[-2:]
    step, steps = pl.program_id(0), w_all.shape[0]

    def piece(index):
        source, shard, slot, row = layout[index]
        first = 0 if row is None else pl.multiple_of(order_ref[steps + row], 128)
        ref = w_hbm[source].at[shard]
        return pltpu.make_async_copy(
            ref, w_all.at[slot, pl.ds(first, ref.shape[0])], arrived.at[slot]
        )

    def block(ref, all_ref, slot, number, sem):
        width = all_ref.shape[2]
        columns = pl.ds(pl.multiple_of(order_ref[number] * width, width), width)
        return pltpu.make_async_copy(ref.at[:, columns], all_ref.at[slot], loaded.at[sem])

    rows_copy = pltpu.make_async_copy(rows_hbm, rows_ref, loaded.at[2 * steps])
    mask_copy = pltpu.make_async_copy(mask_hbm, mask_ref, loaded.at[2 * steps + 1])
    if more:
        before_copy = pltpu.make_async_copy(rest[0], before_ref, loaded.at[2 * steps + 2])

    def ask(slot):
        for index, entry in enumerate(layout):
            if entry[2] == slot:
                piece(index).start()
        block(q_hbm, q_all, slot, slot, slot).start()
        block(g_hbm, g_all, slot, slot, steps + slot).start()

    @pl.when(step == 0)
    def _():
        rows_copy.start()
        ask(0)
        mask_copy.start()
        ask(1)
        acc_ref[...] = jnp.zeros_like(acc_ref)
        rows_copy.wait()
        mask_copy.wait()

    @pl.when(step == 1)
    def _():
        for slot in range(2, steps):
            ask(slot)
        if more:
            before_copy.start()

    pltpu.make_async_copy(w_all.at[step], w_all.at[step], arrived.at[step]).wait()
    pltpu.make_async_copy(q_all.at[step], q_all.at[step], loaded.at[step]).wait()
    pltpu.make_async_copy(g_all.at[step], g_all.at[step], loaded.at[steps + step]).wait()
    q_ref, g_ref = q_all.at[step], g_all.at[step]
    w = w_all[step]
    kv_ref[...] = mm(rows_ref[:, :DC], w, 1, 0).astype(BF16)
    rope_even = rows_ref[:, DC : DC + 128]
    rope_odd = rows_ref[:, DC + 128 :]
    bias = mask_ref[:ROWS, :]
    alive = mask_ref[ROWS : ROWS + 1, :]
    low = lax.broadcasted_iota(jnp.int32, (KEYS, 128), 1) < DR
    staged = []
    for pair in range(HEADS // 2):
        for odd in range(2):
            head = pair * 2 + odd
            at = pair * 384 + odd * 128
            q = q_ref[:, at : at + 256]
            g = g_ref[:, head * 128 : (head + 1) * 128]
            key = kv_ref[:, head * 256 : head * 256 + 128]
            value = kv_ref[:, head * 256 + 128 : (head + 1) * 256]
            if odd:
                turned = jnp.concatenate([key[:, DR:], key[:, :DR]], axis=1)
                zero = jnp.zeros_like(turned)
                key_row = jnp.concatenate(
                    [jnp.where(low, zero, turned), jnp.where(low, turned, rope_odd)], axis=1
                )
            else:
                key_row = jnp.concatenate([key, rope_even], axis=1)
            s = mm(key_row, q, 1, 1)
            s = jnp.concatenate([s[:ROWS], s[ROWS:] + bias], axis=0)
            d_a = mm(value, g, 1, 1)
            staged.append((q, g, value, key_row, s, d_a))
    for pair in range(HEADS // 2):
        merged = None
        for odd in range(2):
            head = pair * 2 + odd
            q, g, value, key_row, s, d_a = staged[head]
            top = jnp.max(s, axis=0, keepdims=True)
            e = jnp.exp2((s - top) * (SCALE * LOG2E))
            inv = alive / jnp.sum(e, axis=0, keepdims=True)
            a_b = (e * inv).astype(BF16)
            delta = jnp.sum(e * d_a, axis=0, keepdims=True) * inv
            d_s = ((e * (d_a - delta)) * (inv * SCALE)).astype(BF16)
            out_ref[:, head * 128 : (head + 1) * 128] = mm(a_b, value, 0, 0).astype(BF16)
            d_q = mm(d_s, key_row, 0, 0)
            if odd:
                dq_ref[:, pair * 384 : pair * 384 + 128] = merged[:, :128].astype(BF16)
                dq_ref[:, pair * 384 + 128 : pair * 384 + 256] = (
                    merged[:, 128:] + d_q[:, :128]
                ).astype(BF16)
                dq_ref[:, pair * 384 + 256 : pair * 384 + 384] = d_q[:, 128:].astype(BF16)
            else:
                merged = d_q
            d_k = mm(d_s, q, 1, 0)
            d_v = mm(a_b, g, 1, 0)
            if odd:
                d_key = jnp.concatenate([d_k[:, DR:128], d_k[:, 128 : 128 + DR]], axis=1)
                acc_ref[:, DC + 128 :] += d_k[:, 128:]
            else:
                d_key = d_k[:, :128]
                acc_ref[:, DC : DC + 128] += d_k[:, 128:]
            dkv_ref[:, head * 256 : head * 256 + 128] = d_key.astype(BF16)
            dkv_ref[:, head * 256 + 128 : (head + 1) * 256] = d_v.astype(BF16)
    acc_ref[:, :DC] += mm(dkv_ref[...], w, 1, 1)


    @pl.when(step == steps - 1)
    def _():
        total = acc_ref[...]
        if more:
            before_copy.wait()
            total += before_ref[...]
        if last:
            rope_sum = total[:, DC : DC + DR] + total[:, DC + 128 + DR :]
            for ref, rows in zip(outs[2:], (slice(0, ROWS), slice(ROWS, KEYS))):
                ref[:, :DC] = total[rows, :DC].astype(BF16)
                ref[:, DC:] = rope_sum[rows].astype(BF16)
        else:
            outs[2][...] = total


def attend(order, rows, mask, weights, layout, queries, grads, before=(), last=False):
    steps = 1 + max(entry[2] for entry in layout)
    split = lambda i, order: (0, order[i])
    args = [order, rows, mask, queries, grads]
    args += list(before[2:]) + list(weights) + list(before[:2])
    aliases = {len(args) - 2: 0, len(args) - 1: 1} if before else {}
    results = [jax.ShapeDtypeStruct((KEYS, 768), F32)]
    if last:
        results = [jax.ShapeDtypeStruct((ROWS, DL), BF16)] * 2
    return pl.pallas_call(
        functools.partial(attend_kernel, layout, int(bool(before)), last),
        grid_spec=pltpu.PrefetchScalarGridSpec(
            num_scalar_prefetch=1,
            grid=(steps,),
            in_specs=[pl.BlockSpec(memory_space=pl.ANY)] * (len(args) - 1),
            out_specs=[
                pl.BlockSpec((ROWS, 512), split),
                pl.BlockSpec((ROWS, 768), split),
            ]
            + [pl.BlockSpec(result.shape, lambda i, order: (0, 0)) for result in results],
            scratch_shapes=[
                pltpu.VMEM((KEYS, 768), BF16),
                pltpu.VMEM((ROWS + 8, 128), F32),
                pltpu.VMEM((steps, ROWS, 768), BF16),
                pltpu.VMEM((steps, ROWS, 512), BF16),
                pltpu.VMEM((steps, DC, 1024), BF16),
                pltpu.VMEM((KEYS, 768), F32),
                pltpu.VMEM((KEYS, 768), F32),
                pltpu.VMEM((KEYS, 1024), BF16),
                pltpu.VMEM((KEYS, 1024), BF16),
                pltpu.SemaphoreType.DMA((steps,)),
                pltpu.SemaphoreType.DMA((2 * steps + 3,)),
            ],
        ),
        out_shape=[
            jax.ShapeDtypeStruct((ROWS, 8192), BF16),
            jax.ShapeDtypeStruct((ROWS, 12288), BF16),
        ]
        + results,
        input_output_aliases=aliases,
        compiler_params=pltpu.CompilerParams(vmem_limit_bytes=VMEM * 1024 * 1024),
        cost_estimate=pl.CostEstimate(
            flops=steps * FLOPS, bytes_accessed=steps * 1_800_000, transcendentals=0
        ),
    )(*args)


def at(x, y, z, core):
    return ((z % 8) * 2 + core) * 16 + (x % 4) * 4 + y % 4


CHIPS = [(x, y, z) for x in range(4) for y in range(4) for z in range(8)]
SWAP = [(at(x, y, z, c), at(x, y, z, 1 - c)) for x, y, z in CHIPS for c in range(2)]


RING = [(at(x, y, z, 0), at(x, y, z + 1, 0)) for x, y, z in CHIPS] + [
    (at(x, y, z, 1), at(x, y, z - 1, 1)) for x, y, z in CHIPS
]
PLANE = [(at(x, y, z, 0), at(x + 1, y, z, 0)) for x, y, z in CHIPS] + [
    (at(x, y, z, 1), at(x, y + 1, z, 1)) for x, y, z in CHIPS
]


def send(a, pairs):
    return lax.ppermute(a, ("prompt", "sample"), pairs)


def places():
    prompt, sample = lax.axis_index("prompt"), lax.axis_index("sample")
    z, core = prompt // 2, prompt % 2
    x, y = sample // 4, sample % 4
    mine = jnp.where(core == 0, x, y)
    other = jnp.where(core == 0, y, x)
    return z, core, mine, other


def after(a, *done):
    return lax.optimization_barrier((a,) + done)[0]


def around(piece):
    local = [piece, send(piece, PLANE)]
    return local + [send(part, SWAP) for part in local]


def layout_of(source, slot, shards):
    return tuple(
        (source + 2 * way + part, shard, slot + way * shards + shard, 2 * way + part)
        for way in (0, 1)
        for shard in range(shards)
        for part in (0, 1)
    )


def body(prompt_latent, resp_latent, queries, d_attended, w_kv, seg_ids, live):
    z, core, mine, other = places()
    prompt = 2 * z + core
    half, other_half = mine % 2 * 256, other % 2 * 256
    pair = [w_kv, send(w_kv, SWAP)]
    here = jnp.stack([lax.dynamic_slice_in_dim(w, half, 256, 0) for w in pair])
    ring = send(here, RING)
    pair = [w[None] for w in pair]
    whole_prompt = lax.all_to_all(
        jnp.tile(after(prompt_latent, here).reshape(-1, DL), (16, 1)), "sample", 0, 0, tiled=True
    )
    rows = jnp.concatenate([whole_prompt, resp_latent.reshape(-1, DL)], axis=0)
    blank = jnp.zeros((KEYS, 128), BF16)
    rows = jnp.concatenate([rows, blank, rows[:, DC:]], axis=1)
    seg = seg_ids[0]
    position = jnp.arange(ROWS, dtype=jnp.int32)
    seen = (
        (seg[:, None] == seg[None, :])
        & (position[:, None] <= position[None, :])
        & (position[:, None] < live[0, 0])
    )
    bias = jnp.where(seen, F32(0.0), F32(-1e30))
    alive = (position < live[0, 0]).astype(F32)[None, :]
    mask = jnp.concatenate([bias, jnp.broadcast_to(alive, (8, ROWS))], axis=0)
    ring, rows, mask = lax.optimization_barrier((ring, rows, mask))
    tensors = (queries[0], d_attended[0])
    starts = jnp.stack([half, 256 - half, other_half, 256 - other_half])
    way = 2 * core - 1

    def order(*steps):
        numbers = []
        for step in steps:
            if step in (0, 4):
                numbers += [2 * ((z + step) % 8) + core, 2 * ((z + step) % 8) + 1 - core]
            else:
                near, far = 2 * ((z + way * step) % 8), 2 * ((z - way * step) % 8)
                numbers += [near + core, near + 1 - core, far + 1 - core, far + core]
        return jnp.concatenate([jnp.stack(numbers), starts]).astype(jnp.int32)

    pair_layout = ((0, 0, 0, None), (1, 0, 1, None))
    results = attend(
        order(0, 1), rows, mask, pair + around(ring), pair_layout + layout_of(2, 2, 2), *tensors
    )
    ring = send(ring, RING)
    second = around(ring)
    ring, before = lax.optimization_barrier((send(ring, RING), results[2]))
    attended, d_queries, prompt_term, resp_term = attend(
        order(2, 3, 4), rows, mask, second + around(ring) + around(send(ring[:1], RING)),
        layout_of(0, 0, 2) + layout_of(4, 4, 2) + layout_of(8, 8, 1),
        *tensors, [*results[:2], before], last=True,
    )
    pieces = lax.all_to_all(prompt_term, "sample", 0, 0, tiled=True).reshape(16, -1, DL)
    d_prompt = jnp.sum(pieces.astype(F32), axis=0).astype(BF16).reshape(1, -1)
    d_resp = resp_term.reshape(1, -1)
    return (attended[None], d_queries[None], d_prompt, d_resp)


def solution(mesh):
    rows = P("prompt", "sample")
    wide = P("prompt", "sample", None)
    return jax.shard_map(
        body,
        mesh=mesh,
        in_specs=(rows, rows, wide, wide, P(None, "prompt"), rows, rows),
        out_specs=(wide, wide, rows, rows),
        check_vma=False,
    )
```

time: 177 us -> 117 us (0.66)
  waiting for transfers between devices: 84.3 us -> 40.5 us
  starting transfers between devices: 6.57 us -> 31.2 us
  blocking collectives: 19.8 us -> 0 us
  between operations: 14.8 us -> 1.49 us
  Pallas kernels: 40.8 us -> 32.3 us
  local copies, waits for them, and re-layouts: 5.52 us -> 8.21 us
  other arithmetic: 4.72 us -> 2.64 us
    all_gather x1 -> x0, waiting for transfers between devices: 77.8 us -> none  [body(): w = lax.all_gather(w_kv, 'prompt', axis=0)]
    ppermute x0 -> x17, waiting for transfers between devices: none -> 30.7 us  [send(): return lax.ppermute(a, ('prompt', 'sample'), pairs)]
    ppermute x0 -> x17, starting transfers between devices: none -> 20 us  [send(): return lax.ppermute(a, ('prompt', 'sample'), pairs)]
    all_gather x1 -> x0, blocking collectives: 19.8 us -> none  [body(): lax.all_gather(prompt_latent, 'sample', axis=1, tiled=True).reshape(-1, DL)]
    pallas_call x1 -> x2, Pallas kernels: 40.8 us -> 32.3 us  [attend(): pl.pallas_call(functools.partial(attend_kernel, layout, int(bool(before))...]
    all_to_all x1 -> x2, starting transfers between devices: 6.53 us -> 11.2 us  [the longest x1 6.75 us: body(): lax.all_to_all(jnp.tile(after(prompt_latent, here).reshape(-1, DL), (16,...]
    all_to_all x1 -> x2, waiting for transfers between devices: 5.81 us -> 9.89 us  [the longest x1 4.98 us: body(): lax.all_to_all(prompt_term, 'sample', 0, 0, tiled=True).reshape(16, -1, DL)]
    another operation x0 -> x4, local copies, waits for them, and re-layouts: none -> 1.89 us  [the longest x2 1.11 us: body(): here = jnp.stack([lax.dynamic_slice_in_dim(w, half, 256, 0) for w in pair])]
  transfers between devices with their start and end apart: 2 -> 19, of which waited for: 2 -> 8; matrix products, arithmetic and copies ran while one was open for 2% -> 7% of each run, Pallas kernels for 0% -> 11%
where the time goes in v2:
time: 117 us; the launch traced here: 116 us
  waiting for transfers between devices  40.5 us (35%)
  Pallas kernels  32.3 us (28%)
  starting transfers between devices  31.2 us (27%)
  local copies, waits for them, and re-layouts  8.21 us (7%)
  other arithmetic  2.64 us (2%)
  between operations  1.49 us (1%)
    pallas_call x2, Pallas kernels, attend(): pl.pallas_call(functools.partial(attend_kernel, layout, int(bool(before))...  32.3 us
    ppermute x17, waiting for transfers between devices, send(): return lax.ppermute(a, ('prompt', 'sample'), pairs)  30.7 us
    ppermute x17, starting transfers between devices, send(): return lax.ppermute(a, ('prompt', 'sample'), pairs)  20 us
    all_to_all x1, starting transfers between devices, body(): lax.all_to_all(jnp.tile(after(prompt_latent, here).reshape(-1, DL), (16,...  6.75 us
    all_to_all x1, waiting for transfers between devices, body(): lax.all_to_all(prompt_term, 'sample', 0, 0, tiled=True).reshape(16, -1, DL)  4.98 us
    all_to_all x1, waiting for transfers between devices, body(): lax.all_to_all(jnp.tile(after(prompt_latent, here).reshape(-1, DL), (16,...  4.91 us
    all_to_all x1, starting transfers between devices, body(): lax.all_to_all(prompt_term, 'sample', 0, 0, tiled=True).reshape(16, -1, DL)  4.45 us
  transfers between devices with their start and end apart: 19, of which 8 were waited for; matrix products, arithmetic and copies ran while one was open for 7% of the time, Pallas kernels for 11%

profile of v2, /device:TPU:1, one launch (start us, length us, event | category | flops | bytes accessed | tf_op | source)
XLA Modules:
  0.0 116.3 jit_solution(14625827323154768261)
XLA Ops:
  0.7 3.3 %collective-permute-start = (bf16[512,1024]{1,0:T(8,128)(2,1)}, bf16[512,1024]{1,0:T(8,128)(2,1)S(1)}, u32[]{:S(2)}, u32[]{:S(2)}) collective-permute-start(bf16[512,1024]{1,0:T(8,128)(2,1)} %param.11), channel_id=1, source_target_pairs={{0,16},{16,0},{32,48},{48,32},{64,80},{80,64},{96,112},{112,96},{1... | collective-permute-start | bytes 3145736 | tf_op jit(solution)/shard_map/ppermute | solution.py:224
  4.0 1.1 dynamic-slice_bitcast_fusion.1
  5.1 1.4 %collective-permute-done = bf16[512,1024]{1,0:T(8,128)(2,1)S(1)} collective-permute-done((bf16[512,1024]{1,0:T(8,128)(2,1)}, bf16[512,1024]{1,0:T(8,128)(2,1)S(1)}, u32[]{:S(2)}, u32[]{:S(2)}) %collective-permute-start) | collective-permute-done | bytes 1048608 | tf_op jit(solution)/shard_map/ppermute | solution.py:224
  6.6 3.9 %collective-permute-start.1 = (bf16[2,256,1024]{2,1,0:T(8,128)(2,1)S(1)}, bf16[2,256,1024]{2,1,0:T(8,128)(2,1)}, u32[]{:S(2)}, u32[]{:S(2)}) collective-permute-start(bf16[2,256,1024]{2,1,0:T(8,128)(2,1)S(1)} %pad_maximum_fusion), channel_id=1, source_target_pairs={{0,32},{32,64},{64,96},{96,128},{128,160},{160,192},{192,224},{224... | collective-permute-start | bytes 3145736 | tf_op jit(solution)/shard_map/ppermute | solution.py:224
  12.1 6.8 %all-to-all-start = ((bf16[16,8,576]{2,1,0:T(8,128)(2,1)}), bf16[16,8,576]{2,1,0:T(8,128)(2,1)S(1)}, u32[]{:S(2)}, u32[]{:S(2)}) async-start(bf16[16,8,576]{2,1,0:T(8,128)(2,1)} %tile.9), calls=%async_computation | async-start | bytes 327680 | tf_op jit(solution)/shard_map/all_to_all | solution.py:262
  19.0 0.9 reduce.3
  20.7 4.9 %all-to-all-done = bf16[16,8,576]{2,1,0:T(8,128)(2,1)S(1)} async-done(((bf16[16,8,576]{2,1,0:T(8,128)(2,1)}), bf16[16,8,576]{2,1,0:T(8,128)(2,1)S(1)}, u32[]{:S(2)}, u32[]{:S(2)}) %all-to-all-start) | async-done | bytes 147488 | tf_op jit(solution)/shard_map/all_to_all | solution.py:262
  26.6 1.2 %collective-permute-start.2 = (bf16[2,256,1024]{2,1,0:T(8,128)(2,1)}, bf16[2,256,1024]{2,1,0:T(8,128)(2,1)S(1)}, u32[]{:S(2)}, u32[]{:S(2)}) collective-permute-start(bf16[2,256,1024]{2,1,0:T(8,128)(2,1)} %collective-permute-done.1.rest_2_), channel_id=1, source_target_pairs={{0,32},{32,64},{64,96},{96,128},{128,160},{160,192},{192,224},{224... | collective-permute-start | bytes 3145736 | tf_op jit(solution)/shard_map/ppermute | solution.py:224
  27.9 13.9 %collective-permute-done.4.rest_3_ = bf16[2,256,1024]{2,1,0:T(8,128)(2,1)} collective-permute-done((bf16[2,256,1024]{2,1,0:T(8,128)(2,1)}, bf16[2,256,1024]{2,1,0:T(8,128)(2,1)}, u32[]{:S(2)}, u32[]{:S(2)}) %collective-permute-start.4) | collective-permute-done | bytes 1048608 | tf_op jit(solution)/shard_map/ppermute | solution.py:224
  42.5 3.5 %collective-permute-start.3 = (bf16[2,256,1024]{2,1,0:T(8,128)(2,1)S(1)}, bf16[2,256,1024]{2,1,0:T(8,128)(2,1)S(1)}, u32[]{:S(2)}, u32[]{:S(2)}) collective-permute-start(bf16[2,256,1024]{2,1,0:T(8,128)(2,1)S(1)} %collective-permute-done.2.rest_1_), channel_id=1, source_target_pairs={{0,32},{32,64},{64,96},{96,128},{128,160},{160,192},{192,224},{224... | collective-permute-start | bytes 3145736 | tf_op jit(solution)/shard_map/ppermute | solution.py:224
  46.1 12.9 %shard_map.102 = (bf16[128,8192]{1,0:T(8,128)(2,1)}, bf16[128,12288]{1,0:T(8,128)(2,1)}, f32[256,768]{1,0:T(8,128)}) custom-call(s32[10]{0:T(128)} %concatenate.21.order_ref, bf16[256,768]{1,0:T(8,128)(2,1)} %fusion.3.rows_hbm, f32[136,128]{1,0:T(8,128)} %pad_maximum_fusion.1.mask_hbm, bf16[128,12288]{1,0:T(8,128)(2,1)} %bitcast.40, ...), custom_call_target="tpu_custom_call" | custom-call | flops 24000000000 | bytes 10800000 | tf_op jit(solution)/shard_map/pallas_call | solution.py:169
  60.7 1.2 %collective-permute-start.13 = (bf16[1,256,1024]{2,1,0:T(8,128)(2,1)S(1)}, bf16[1,256,1024]{2,1,0:T(8,128)(2,1)}, u32[]{:S(2)}, u32[]{:S(2)}) collective-permute-start(bf16[1,256,1024]{2,1,0:T(8,128)(2,1)S(1)} %slice.7), channel_id=1, source_target_pairs={{0,32},{32,64},{64,96},{96,128},{128,160},{160,192},{192,224},{224... | collective-permute-start | bytes 1572872 | tf_op jit(solution)/shard_map/ppermute | solution.py:224
  62.4 6.7 %collective-permute-done.13.rest_9_ = bf16[1,256,1024]{2,1,0:T(8,128)(2,1)} collective-permute-done((bf16[1,256,1024]{2,1,0:T(8,128)(2,1)S(1)}, bf16[1,256,1024]{2,1,0:T(8,128)(2,1)}, u32[]{:S(2)}, u32[]{:S(2)}) %collective-permute-start.13) | collective-permute-done | bytes 524320 | tf_op jit(solution)/shard_map/ppermute | solution.py:224
  69.2 1.2 %collective-permute-start.14 = (bf16[1,256,1024]{2,1,0:T(8,128)(2,1)}, bf16[1,256,1024]{2,1,0:T(8,128)(2,1)}, u32[]{:S(2)}, u32[]{:S(2)}) collective-permute-start(bf16[1,256,1024]{2,1,0:T(8,128)(2,1)} %collective-permute-done.13.rest_9_), channel_id=1, source_target_pairs={{0,4},{32,36},{64,68},{96,100},{128,132},{160,164},{192,196},{224,... | collective-permute-start | bytes 1572872 | tf_op jit(solution)/shard_map/ppermute | solution.py:224
  70.4 4.0 %collective-permute-done.10.rest_6_ = bf16[2,256,1024]{2,1,0:T(8,128)(2,1)} collective-permute-done((bf16[2,256,1024]{2,1,0:T(8,128)(2,1)S(1)}, bf16[2,256,1024]{2,1,0:T(8,128)(2,1)}, u32[]{:S(2)}, u32[]{:S(2)}) %collective-permute-start.10) | collective-permute-done | bytes 1048608 | tf_op jit(solution)/shard_map/ppermute | solution.py:224
  74.4 1.3 %collective-permute-start.12 = (bf16[2,256,1024]{2,1,0:T(8,128)(2,1)}, bf16[2,256,1024]{2,1,0:T(8,128)(2,1)S(1)}, u32[]{:S(2)}, u32[]{:S(2)}) collective-permute-start(bf16[2,256,1024]{2,1,0:T(8,128)(2,1)} %collective-permute-done.10.rest_6_), channel_id=1, source_target_pairs={{0,16},{16,0},{32,48},{48,32},{64,80},{80,64},{96,112},{112,96},{1... | collective-permute-start | bytes 3145736 | tf_op jit(solution)/shard_map/ppermute | solution.py:224
  75.6 1.0 copy-done.6
  76.6 3.4 %collective-permute-done.14.rest_10_ = bf16[1,256,1024]{2,1,0:T(8,128)(2,1)} collective-permute-done((bf16[1,256,1024]{2,1,0:T(8,128)(2,1)}, bf16[1,256,1024]{2,1,0:T(8,128)(2,1)}, u32[]{:S(2)}, u32[]{:S(2)}) %collective-permute-start.14) | collective-permute-done | bytes 524320 | tf_op jit(solution)/shard_map/ppermute | solution.py:224
  80.0 2.0 %collective-permute-start.16 = (bf16[1,256,1024]{2,1,0:T(8,128)(2,1)}, bf16[1,256,1024]{2,1,0:T(8,128)(2,1)S(1)}, u32[]{:S(2)}, u32[]{:S(2)}) collective-permute-start(bf16[1,256,1024]{2,1,0:T(8,128)(2,1)} %collective-permute-done.14.rest_10_), channel_id=1, source_target_pairs={{0,16},{16,0},{32,48},{48,32},{64,80},{80,64},{96,112},{112,96},{1... | collective-permute-start | bytes 1572872 | tf_op jit(solution)/shard_map/ppermute | solution.py:224
  82.5 1.1 collective-permute-done.16.rest_12_
  84.9 19.3 %shard_map.103 = (bf16[128,8192]{1,0:T(8,128)(2,1)}, bf16[128,12288]{1,0:T(8,128)(2,1)}, bf16[128,576]{1,0:T(8,128)(2,1)}, bf16[128,576]{1,0:T(8,128)(2,1)}) custom-call(s32[14]{0:T(128)} %concatenate.17.order_ref, bf16[256,768]{1,0:T(8,128)(2,1)} %fusion.3.rows_hbm, ...), custom_call_target="tpu_custom_call", output_to_operand_aliasing={{0}: (18, {}), {1}: (19, {})} | custom-call | flops 40000000000 | bytes 18000000 | tf_op jit(solution)/shard_map/pallas_call | solution.py:169
  104.3 4.5 %all-to-all-start.1 = ((bf16[16,8,576]{2,1,0:T(8,128)(2,1)}), bf16[16,8,576]{2,1,0:T(8,128)(2,1)S(1)}, u32[]{:S(2)}, u32[]{:S(2)}) async-start(bf16[16,8,576]{2,1,0:T(8,128)(2,1)} %bitcast.38), calls=%async_computation.1 | async-start | bytes 327680 | tf_op jit(solution)/shard_map/all_to_all | solution.py:305
  108.7 1.9 %reshape.41 = bf16[1,73728]{1,0:T(2,128)(2,1)} reshape(bf16[128,576]{1,0:T(8,128)(2,1)} %get-tuple-element.29) | data formatting | bytes 294912 | tf_op jit(solution)/shard_map/reshape | solution.py:307
  110.6 5.0 %all-to-all-done.1 = bf16[16,8,576]{2,1,0:T(8,128)(2,1)S(1)} async-done(((bf16[16,8,576]{2,1,0:T(8,128)(2,1)}), bf16[16,8,576]{2,1,0:T(8,128)(2,1)S(1)}, u32[]{:S(2)}, u32[]{:S(2)}) %all-to-all-start.1) | async-done | bytes 147488 | tf_op jit(solution)/shard_map/all_to_all | solution.py:305
  (57 shorter events, 8.4 us)
Async XLA Ops:
  0.6 18.2 %copy-start.4 = (s32[1,128]{1,0:T(1,128)S(1)}, s32[1,128]{1,0:T(1,128)}, u32[]{:S(2)}) copy-start(s32[1,128]{1,0:T(1,128)} %param.12) | copy-start | bytes 1540
  0.7 18.3 %copy-start = (bf16[1,73728]{1,0:T(2,128)(2,1)S(1)}, bf16[1,73728]{1,0:T(2,128)(2,1)}, u32[]{:S(2)}) copy-start(bf16[1,73728]{1,0:T(2,128)(2,1)} %param.8) | copy-start | bytes 442372
  0.7 5.8 %collective-permute-start = (bf16[512,1024]{1,0:T(8,128)(2,1)}, bf16[512,1024]{1,0:T(8,128)(2,1)S(1)}, u32[]{:S(2)}, u32[]{:S(2)}) collective-permute-start(bf16[512,1024]{1,0:T(8,128)(2,1)} %param.11), channel_id=1, source_target_pairs={{0,16},{16,0},{32,48},{48,32},{64,80},{80,64},{96,112},{112,96},{1... | collective-permute-start | bytes 3145736 | tf_op jit(solution)/shard_map/ppermute | solution.py:224
  6.5 39.6 %copy-start.2 = (bf16[512,1024]{1,0:T(8,128)(2,1)}, bf16[512,1024]{1,0:T(8,128)(2,1)S(1)}, u32[]{:S(2)}) copy-start(bf16[512,1024]{1,0:T(8,128)(2,1)S(1)} %collective-permute-done) | copy-start | bytes 3145732
  6.6 19.8 %collective-permute-start.1 = (bf16[2,256,1024]{2,1,0:T(8,128)(2,1)S(1)}, bf16[2,256,1024]{2,1,0:T(8,128)(2,1)}, u32[]{:S(2)}, u32[]{:S(2)}) collective-permute-start(bf16[2,256,1024]{2,1,0:T(8,128)(2,1)S(1)} %pad_maximum_fusion), channel_id=1, source_target_pairs={{0,32},{32,64},{64,96},{96,128},{128,160},{160,192},{192,224},{224... | collective-permute-start | bytes 3145736 | tf_op jit(solution)/shard_map/ppermute | solution.py:224
  12.1 13.6 %all-to-all-start = ((bf16[16,8,576]{2,1,0:T(8,128)(2,1)}), bf16[16,8,576]{2,1,0:T(8,128)(2,1)S(1)}, u32[]{:S(2)}, u32[]{:S(2)}) async-start(bf16[16,8,576]{2,1,0:T(8,128)(2,1)} %tile.9), calls=%async_computation | async-start | bytes 327680 | tf_op jit(solution)/shard_map/all_to_all | solution.py:262
  26.5 15.4 %collective-permute-start.4 = (bf16[2,256,1024]{2,1,0:T(8,128)(2,1)}, bf16[2,256,1024]{2,1,0:T(8,128)(2,1)}, u32[]{:S(2)}, u32[]{:S(2)}) collective-permute-start(bf16[2,256,1024]{2,1,0:T(8,128)(2,1)} %collective-permute-done.1.rest_2_), channel_id=1, source_target_pairs={{0,4},{32,36},{64,68},{96,100},{128,132},{160,164},{192,196},{224,... | collective-permute-start | bytes 3145736 | tf_op jit(solution)/shard_map/ppermute | solution.py:224
  26.6 15.9 %collective-permute-start.2 = (bf16[2,256,1024]{2,1,0:T(8,128)(2,1)}, bf16[2,256,1024]{2,1,0:T(8,128)(2,1)S(1)}, u32[]{:S(2)}, u32[]{:S(2)}) collective-permute-start(bf16[2,256,1024]{2,1,0:T(8,128)(2,1)} %collective-permute-done.1.rest_2_), channel_id=1, source_target_pairs={{0,32},{32,64},{64,96},{96,128},{128,160},{160,192},{192,224},{224... | collective-permute-start | bytes 3145736 | tf_op jit(solution)/shard_map/ppermute | solution.py:224
  27.9 18.2 %collective-permute-start.5 = (bf16[2,256,1024]{2,1,0:T(8,128)(2,1)}, bf16[2,256,1024]{2,1,0:T(8,128)(2,1)}, u32[]{:S(2)}, u32[]{:S(2)}) collective-permute-start(bf16[2,256,1024]{2,1,0:T(8,128)(2,1)} %collective-permute-done.1.rest_2_), channel_id=1, source_target_pairs={{0,16},{16,0},{32,48},{48,32},{64,80},{80,64},{96,112},{112,96},{1... | collective-permute-start | bytes 3145736 | tf_op jit(solution)/shard_map/ppermute | solution.py:224
  41.8 4.2 %collective-permute-start.6 = (bf16[2,256,1024]{2,1,0:T(8,128)(2,1)}, bf16[2,256,1024]{2,1,0:T(8,128)(2,1)}, u32[]{:S(2)}, u32[]{:S(2)}) collective-permute-start(bf16[2,256,1024]{2,1,0:T(8,128)(2,1)} %collective-permute-done.4.rest_3_), channel_id=1, source_target_pairs={{0,16},{16,0},{32,48},{48,32},{64,80},{80,64},{96,112},{112,96},{1... | collective-permute-start | bytes 3145736 | tf_op jit(solution)/shard_map/ppermute | solution.py:224
  42.5 17.3 %copy-start.5 = (bf16[2,256,1024]{2,1,0:T(8,128)(2,1)}, bf16[2,256,1024]{2,1,0:T(8,128)(2,1)S(1)}, u32[]{:S(2)}) copy-start(bf16[2,256,1024]{2,1,0:T(8,128)(2,1)S(1)} %collective-permute-done.2.rest_1_) | copy-start | bytes 3145732
  42.5 19.4 %collective-permute-start.7 = (bf16[2,256,1024]{2,1,0:T(8,128)(2,1)S(1)}, bf16[2,256,1024]{2,1,0:T(8,128)(2,1)}, u32[]{:S(2)}, u32[]{:S(2)}) collective-permute-start(bf16[2,256,1024]{2,1,0:T(8,128)(2,1)S(1)} %collective-permute-done.2.rest_1_), channel_id=1, source_target_pairs={{0,4},{32,36},{64,68},{96,100},{128,132},{160,164},{192,196},{224,... | collective-permute-start | bytes 3145736 | tf_op jit(solution)/shard_map/ppermute | solution.py:224
  42.5 16.5 %collective-permute-start.3 = (bf16[2,256,1024]{2,1,0:T(8,128)(2,1)S(1)}, bf16[2,256,1024]{2,1,0:T(8,128)(2,1)S(1)}, u32[]{:S(2)}, u32[]{:S(2)}) collective-permute-start(bf16[2,256,1024]{2,1,0:T(8,128)(2,1)S(1)} %collective-permute-done.2.rest_1_), channel_id=1, source_target_pairs={{0,32},{32,64},{64,96},{96,128},{128,160},{160,192},{192,224},{224... | collective-permute-start | bytes 3145736 | tf_op jit(solution)/shard_map/ppermute | solution.py:224
  59.0 24.7 %copy-start.1 = (bf16[2,256,1024]{2,1,0:T(8,128)(2,1)}, bf16[2,256,1024]{2,1,0:T(8,128)(2,1)S(1)}, u32[]{:S(2)}) copy-start(bf16[2,256,1024]{2,1,0:T(8,128)(2,1)S(1)} %collective-permute-done.3.rest_5_) | copy-start | bytes 3145732
  59.0 15.3 %collective-permute-start.10 = (bf16[2,256,1024]{2,1,0:T(8,128)(2,1)S(1)}, bf16[2,256,1024]{2,1,0:T(8,128)(2,1)}, u32[]{:S(2)}, u32[]{:S(2)}) collective-permute-start(bf16[2,256,1024]{2,1,0:T(8,128)(2,1)S(1)} %collective-permute-done.3.rest_5_), channel_id=1, source_target_pairs={{0,4},{32,36},{64,68},{96,100},{128,132},{160,164},{192,196},{224,... | collective-permute-start | bytes 3145736 | tf_op jit(solution)/shard_map/ppermute | solution.py:224
  59.8 15.8 %collective-permute-start.8 = (bf16[2,256,1024]{2,1,0:T(8,128)(2,1)S(1)}, bf16[2,256,1024]{2,1,0:T(8,128)(2,1)S(1)}, u32[]{:S(2)}, u32[]{:S(2)}) collective-permute-start(bf16[2,256,1024]{2,1,0:T(8,128)(2,1)S(1)} %collective-permute-done.2.rest_1_), channel_id=1, source_target_pairs={{0,16},{16,0},{32,48},{48,32},{64,80},{80,64},{96,112},{112,96},{1... | collective-permute-start | bytes 3145736 | tf_op jit(solution)/shard_map/ppermute | solution.py:224
  60.7 8.5 %collective-permute-start.13 = (bf16[1,256,1024]{2,1,0:T(8,128)(2,1)S(1)}, bf16[1,256,1024]{2,1,0:T(8,128)(2,1)}, u32[]{:S(2)}, u32[]{:S(2)}) collective-permute-start(bf16[1,256,1024]{2,1,0:T(8,128)(2,1)S(1)} %slice.7), channel_id=1, source_target_pairs={{0,32},{32,64},{64,96},{96,128},{128,160},{160,192},{192,224},{224... | collective-permute-start | bytes 1572872 | tf_op jit(solution)/shard_map/ppermute | solution.py:224
  61.9 20.6 %collective-permute-start.11 = (bf16[2,256,1024]{2,1,0:T(8,128)(2,1)S(1)}, bf16[2,256,1024]{2,1,0:T(8,128)(2,1)}, u32[]{:S(2)}, u32[]{:S(2)}) collective-permute-start(bf16[2,256,1024]{2,1,0:T(8,128)(2,1)S(1)} %collective-permute-done.3.rest_5_), channel_id=1, source_target_pairs={{0,16},{16,0},{32,48},{48,32},{64,80},{80,64},{96,112},{112,96},{1... | collective-permute-start | bytes 3145736 | tf_op jit(solution)/shard_map/ppermute | solution.py:224
  61.9 20.6 %collective-permute-start.9 = (bf16[2,256,1024]{2,1,0:T(8,128)(2,1)}, bf16[2,256,1024]{2,1,0:T(8,128)(2,1)}, u32[]{:S(2)}, u32[]{:S(2)}) collective-permute-start(bf16[2,256,1024]{2,1,0:T(8,128)(2,1)} %collective-permute-done.7.rest_2_), channel_id=1, source_target_pairs={{0,16},{16,0},{32,48},{48,32},{64,80},{80,64},{96,112},{112,96},{1... | collective-permute-start | bytes 3145736 | tf_op jit(solution)/shard_map/ppermute | solution.py:224
  69.2 10.8 %collective-permute-start.14 = (bf16[1,256,1024]{2,1,0:T(8,128)(2,1)}, bf16[1,256,1024]{2,1,0:T(8,128)(2,1)}, u32[]{:S(2)}, u32[]{:S(2)}) collective-permute-start(bf16[1,256,1024]{2,1,0:T(8,128)(2,1)} %collective-permute-done.13.rest_9_), channel_id=1, source_target_pairs={{0,4},{32,36},{64,68},{96,100},{128,132},{160,164},{192,196},{224,... | collective-permute-start | bytes 1572872 | tf_op jit(solution)/shard_map/ppermute | solution.py:224
  74.4 9.3 %collective-permute-start.12 = (bf16[2,256,1024]{2,1,0:T(8,128)(2,1)}, bf16[2,256,1024]{2,1,0:T(8,128)(2,1)S(1)}, u32[]{:S(2)}, u32[]{:S(2)}) collective-permute-start(bf16[2,256,1024]{2,1,0:T(8,128)(2,1)} %collective-permute-done.10.rest_6_), channel_id=1, source_target_pairs={{0,16},{16,0},{32,48},{48,32},{64,80},{80,64},{96,112},{112,96},{1... | collective-permute-start | bytes 3145736 | tf_op jit(solution)/shard_map/ppermute | solution.py:224
  76.6 5.9 %collective-permute-start.15 = (bf16[1,256,1024]{2,1,0:T(8,128)(2,1)}, bf16[1,256,1024]{2,1,0:T(8,128)(2,1)S(1)}, u32[]{:S(2)}, u32[]{:S(2)}) collective-permute-start(bf16[1,256,1024]{2,1,0:T(8,128)(2,1)} %collective-permute-done.13.rest_9_), channel_id=1, source_target_pairs={{0,16},{16,0},{32,48},{48,32},{64,80},{80,64},{96,112},{112,96},{1... | collective-permute-start | bytes 1572872 | tf_op jit(solution)/shard_map/ppermute | solution.py:224
  80.0 3.7 %collective-permute-start.16 = (bf16[1,256,1024]{2,1,0:T(8,128)(2,1)}, bf16[1,256,1024]{2,1,0:T(8,128)(2,1)S(1)}, u32[]{:S(2)}, u32[]{:S(2)}) collective-permute-start(bf16[1,256,1024]{2,1,0:T(8,128)(2,1)} %collective-permute-done.14.rest_10_), channel_id=1, source_target_pairs={{0,16},{16,0},{32,48},{48,32},{64,80},{80,64},{96,112},{112,96},{1... | collective-permute-start | bytes 1572872 | tf_op jit(solution)/shard_map/ppermute | solution.py:224
  104.3 11.3 %all-to-all-start.1 = ((bf16[16,8,576]{2,1,0:T(8,128)(2,1)}), bf16[16,8,576]{2,1,0:T(8,128)(2,1)S(1)}, u32[]{:S(2)}, u32[]{:S(2)}) async-start(bf16[16,8,576]{2,1,0:T(8,128)(2,1)} %bitcast.38), calls=%async_computation.1 | async-start | bytes 327680 | tf_op jit(solution)/shard_map/all_to_all | solution.py:305
  (5 other events, 14.8 us)

commit v3 on v2

--- a/solution.py
+++ b/solution.py
@@ -64,21 +64,21 @@
         rows_copy.start()
         ask(0)
         mask_copy.start()
-        ask(1)
         acc_ref[...] = jnp.zeros_like(acc_ref)
         rows_copy.wait()
         mask_copy.wait()
 
-    @pl.when(step == 1)
+    pltpu.make_async_copy(w_all.at[step], w_all.at[step], arrived.at[step]).wait()
+    pltpu.make_async_copy(q_all.at[step], q_all.at[step], loaded.at[step]).wait()
+    pltpu.make_async_copy(g_all.at[step], g_all.at[step], loaded.at[steps + step]).wait()
+
+    @pl.when(step == 0)
     def _():
-        for slot in range(2, steps):
+        for slot in range(1, steps):
             ask(slot)
         if more:
             before_copy.start()
 
-    pltpu.make_async_copy(w_all.at[step], w_all.at[step], arrived.at[step]).wait()
-    pltpu.make_async_copy(q_all.at[step], q_all.at[step], loaded.at[step]).wait()
-    pltpu.make_async_copy(g_all.at[step], g_all.at[step], loaded.at[steps + step]).wait()
     q_ref, g_ref = q_all.at[step], g_all.at[step]
     w = w_all[step]
     kv_ref[...] = mm(rows_ref[:, :DC], w, 1, 0).astype(BF16)
@@ -237,9 +237,8 @@
     return lax.optimization_barrier((a,) + done)[0]
 
 
-def around(piece):
-    local = [piece, send(piece, PLANE)]
-    return local + [send(part, SWAP) for part in local]
+def with_other_core(piece, rest):
+    return [piece, rest, send(piece, SWAP), send(rest, SWAP)]
 
 
 def layout_of(source, slot, shards):
@@ -291,14 +290,22 @@
         return jnp.concatenate([jnp.stack(numbers), starts]).astype(jnp.int32)
 
     pair_layout = ((0, 0, 0, None), (1, 0, 1, None))
+    results = attend(order(0), rows, mask, pair, pair_layout, *tensors)
+    rest1, ring2, before = lax.optimization_barrier(
+        (send(ring, PLANE), send(ring, RING), results[2])
+    )
     results = attend(
-        order(0, 1), rows, mask, pair + around(ring), pair_layout + layout_of(2, 2, 2), *tensors
-    )
-    ring = send(ring, RING)
-    second = around(ring)
-    ring, before = lax.optimization_barrier((send(ring, RING), results[2]))
+        order(1), rows, mask, with_other_core(ring, rest1), layout_of(0, 0, 2),
+        *tensors, [*results[:2], before],
+    )
+    second = with_other_core(ring2, send(ring2, PLANE))
+    ring3, before = lax.optimization_barrier((send(ring2, RING), results[2]))
+    ring4 = send(ring3[:1], RING)
+    rest3, rest4 = lax.optimization_barrier((send(ring3, PLANE), send(ring4, PLANE)))
+    third = with_other_core(ring3, rest3)
+    fourth = with_other_core(ring4, rest4)
     attended, d_queries, prompt_term, resp_term = attend(
-        order(2, 3, 4), rows, mask, second + around(ring) + around(send(ring[:1], RING)),
+        order(2, 3, 4), rows, mask, second + third + fourth,
         layout_of(0, 0, 2) + layout_of(4, 4, 2) + layout_of(8, 8, 1),
         *tensors, [*results[:2], before], last=True,
     )

time: 117 us -> 120 us (1.026)
  Pallas kernels: 32.3 us -> 35.7 us
  waiting for transfers between devices: 40.5 us -> 38.5 us
    pallas_call x2 -> x3, Pallas kernels: 32.3 us -> 35.7 us  [attend(): pl.pallas_call(functools.partial(attend_kernel, layout, int(bool(before))...]
    ppermute x17, waiting for transfers between devices: 30.7 us -> 28.6 us  [send(): return lax.ppermute(a, ('prompt', 'sample'), pairs)]
  transfers between devices with their start and end apart: 19 -> 19, of which waited for: 8 -> 10; matrix products, arithmetic and copies ran while one was open for 7% -> 7% of each run, Pallas kernels for 11% -> 14%
where the time goes in v3:
time: 120 us; the launch traced here: 119 us
  waiting for transfers between devices  38.5 us (32%)
  Pallas kernels  35.7 us (30%)
  starting transfers between devices  31.8 us (26%)
  local copies, waits for them, and re-layouts  8.45 us (7%)
  other arithmetic  2.64 us (2%)
  between operations  1.46 us (1%)
    pallas_call x3, Pallas kernels, attend(): pl.pallas_call(functools.partial(attend_kernel, layout, int(bool(before))...  35.7 us
    ppermute x17, waiting for transfers between devices, send(): return lax.ppermute(a, ('prompt', 'sample'), pairs)  28.6 us
    ppermute x17, starting transfers between devices, send(): return lax.ppermute(a, ('prompt', 'sample'), pairs)  20.9 us
    all_to_all x1, starting transfers between devices, body(): lax.all_to_all(jnp.tile(after(prompt_latent, here).reshape(-1, DL), (16,...  6.75 us
    all_to_all x1, waiting for transfers between devices, body(): lax.all_to_all(prompt_term, 'sample', 0, 0, tiled=True).reshape(16, -1, DL)  4.97 us
    all_to_all x1, waiting for transfers between devices, body(): lax.all_to_all(jnp.tile(after(prompt_latent, here).reshape(-1, DL), (16,...  4.91 us
    all_to_all x1, starting transfers between devices, body(): lax.all_to_all(prompt_term, 'sample', 0, 0, tiled=True).reshape(16, -1, DL)  4.14 us
  transfers between devices with their start and end apart: 19, of which 10 were waited for; matrix products, arithmetic and copies ran while one was open for 7% of the time, Pallas kernels for 14%

profile of v3, /device:TPU:1, one launch (start us, length us, event | category | flops | bytes accessed | tf_op | source)
XLA Modules:
  0.0 118.6 jit_solution(11357764575609656994)
XLA Ops:
  0.7 3.3 %collective-permute-start = (bf16[512,1024]{1,0:T(8,128)(2,1)}, bf16[512,1024]{1,0:T(8,128)(2,1)S(1)}, u32[]{:S(2)}, u32[]{:S(2)}) collective-permute-start(bf16[512,1024]{1,0:T(8,128)(2,1)} %param.11), channel_id=1, source_target_pairs={{0,16},{16,0},{32,48},{48,32},{64,80},{80,64},{96,112},{112,96},{1... | collective-permute-start | bytes 3145736 | tf_op jit(solution)/shard_map/ppermute | solution.py:224
  4.0 1.1 dynamic-slice_bitcast_fusion.1
  5.1 1.4 %collective-permute-done = bf16[512,1024]{1,0:T(8,128)(2,1)S(1)} collective-permute-done((bf16[512,1024]{1,0:T(8,128)(2,1)}, bf16[512,1024]{1,0:T(8,128)(2,1)S(1)}, u32[]{:S(2)}, u32[]{:S(2)}) %collective-permute-start) | collective-permute-done | bytes 1048608 | tf_op jit(solution)/shard_map/ppermute | solution.py:224
  6.6 3.9 %collective-permute-start.1 = (bf16[2,256,1024]{2,1,0:T(8,128)(2,1)S(1)}, bf16[2,256,1024]{2,1,0:T(8,128)(2,1)}, u32[]{:S(2)}, u32[]{:S(2)}) collective-permute-start(bf16[2,256,1024]{2,1,0:T(8,128)(2,1)S(1)} %pad_maximum_fusion), channel_id=1, source_target_pairs={{0,32},{32,64},{64,96},{96,128},{128,160},{160,192},{192,224},{224... | collective-permute-start | bytes 3145736 | tf_op jit(solution)/shard_map/ppermute | solution.py:224
  12.1 6.8 %all-to-all-start = ((bf16[16,8,576]{2,1,0:T(8,128)(2,1)}), bf16[16,8,576]{2,1,0:T(8,128)(2,1)S(1)}, u32[]{:S(2)}, u32[]{:S(2)}) async-start(bf16[16,8,576]{2,1,0:T(8,128)(2,1)} %tile.9), calls=%async_computation | async-start | bytes 327680 | tf_op jit(solution)/shard_map/all_to_all | solution.py:261
  19.0 0.9 reduce.3
  20.7 4.9 %all-to-all-done = bf16[16,8,576]{2,1,0:T(8,128)(2,1)S(1)} async-done(((bf16[16,8,576]{2,1,0:T(8,128)(2,1)}), bf16[16,8,576]{2,1,0:T(8,128)(2,1)S(1)}, u32[]{:S(2)}, u32[]{:S(2)}) %all-to-all-start) | async-done | bytes 147488 | tf_op jit(solution)/shard_map/all_to_all | solution.py:261
  26.5 1.3 %collective-permute-start.3 = (bf16[2,256,1024]{2,1,0:T(8,128)(2,1)}, bf16[2,256,1024]{2,1,0:T(8,128)(2,1)S(1)}, u32[]{:S(2)}, u32[]{:S(2)}) collective-permute-start(bf16[2,256,1024]{2,1,0:T(8,128)(2,1)} %collective-permute-done.1.rest_1_), channel_id=1, source_target_pairs={{0,32},{32,64},{64,96},{96,128},{128,160},{160,192},{192,224},{224... | collective-permute-start | bytes 3145736 | tf_op jit(solution)/shard_map/ppermute | solution.py:224
  28.6 6.4 %shard_map.102 = (bf16[128,8192]{1,0:T(8,128)(2,1)}, bf16[128,12288]{1,0:T(8,128)(2,1)}, f32[256,768]{1,0:T(8,128)}) custom-call(s32[6]{0:T(128)} %concatenate.25.order_ref, bf16[256,768]{1,0:T(8,128)(2,1)} %fusion.3.rows_hbm, f32[136,128]{1,0:T(8,128)} %pad_maximum_fusion.1.mask_hbm, bf16[128,12288]{1,0:T(8,128)(2,1)} %bitcast.40, ...), custom_call_target="tpu_custom_call" | custom-call | flops 8000000000 | bytes 3600000 | tf_op jit(solution)/shard_map/pallas_call | solution.py:169
  34.9 5.8 %collective-permute-done.3.rest_1_ = bf16[2,256,1024]{2,1,0:T(8,128)(2,1)S(1)} collective-permute-done((bf16[2,256,1024]{2,1,0:T(8,128)(2,1)}, bf16[2,256,1024]{2,1,0:T(8,128)(2,1)S(1)}, u32[]{:S(2)}, u32[]{:S(2)}) %collective-permute-start.3) | collective-permute-done | bytes 1048608 | tf_op jit(solution)/shard_map/ppermute | solution.py:224
  40.7 2.2 %collective-permute-done.2.rest_2_ = bf16[2,256,1024]{2,1,0:T(8,128)(2,1)} collective-permute-done((bf16[2,256,1024]{2,1,0:T(8,128)(2,1)}, bf16[2,256,1024]{2,1,0:T(8,128)(2,1)}, u32[]{:S(2)}, u32[]{:S(2)}) %collective-permute-start.2) | collective-permute-done | bytes 1048608 | tf_op jit(solution)/shard_map/ppermute | solution.py:224
  43.7 2.3 %collective-permute-start.4 = (bf16[2,256,1024]{2,1,0:T(8,128)(2,1)S(1)}, bf16[2,256,1024]{2,1,0:T(8,128)(2,1)S(1)}, u32[]{:S(2)}, u32[]{:S(2)}) collective-permute-start(bf16[2,256,1024]{2,1,0:T(8,128)(2,1)S(1)} %collective-permute-done.3.rest_1_), channel_id=1, source_target_pairs={{0,32},{32,64},{64,96},{96,128},{128,160},{160,192},{192,224},{224... | collective-permute-start | bytes 3145736 | tf_op jit(solution)/shard_map/ppermute | solution.py:224
  46.1 10.1 %shard_map.103 = (bf16[128,8192]{1,0:T(8,128)(2,1)}, bf16[128,12288]{1,0:T(8,128)(2,1)}, f32[256,768]{1,0:T(8,128)}) custom-call(s32[8]{0:T(128)} %concatenate.26.order_ref, bf16[256,768]{1,0:T(8,128)(2,1)} %fusion.3.rows_hbm, f32[136,128]{1,0:T(8,128)} %pad_maximum_fusion.1.mask_hbm, ...), custom_call_target="tpu_custom_call", output_to_operand_aliasing={{0}: (10, {}), {1}: (11, {})} | custom-call | flops 16000000000 | bytes 7200000 | tf_op jit(solution)/shard_map/pallas_call | solution.py:169
  56.1 1.7 %collective-permute-done.4.rest_5_ = bf16[2,256,1024]{2,1,0:T(8,128)(2,1)S(1)} collective-permute-done((bf16[2,256,1024]{2,1,0:T(8,128)(2,1)S(1)}, bf16[2,256,1024]{2,1,0:T(8,128)(2,1)S(1)}, u32[]{:S(2)}, u32[]{:S(2)}) %collective-permute-start.4) | collective-permute-done | bytes 1048608 | tf_op jit(solution)/shard_map/ppermute | solution.py:224
  57.9 3.4 %collective-permute-start.11 = (bf16[1,256,1024]{2,1,0:T(8,128)(2,1)S(1)}, bf16[1,256,1024]{2,1,0:T(8,128)(2,1)}, u32[]{:S(2)}, u32[]{:S(2)}) collective-permute-start(bf16[1,256,1024]{2,1,0:T(8,128)(2,1)S(1)} %slice.7), channel_id=1, source_target_pairs={{0,32},{32,64},{64,96},{96,128},{128,160},{160,192},{192,224},{224... | collective-permute-start | bytes 1572872 | tf_op jit(solution)/shard_map/ppermute | solution.py:224
  61.8 6.0 %collective-permute-done.11.rest_9_ = bf16[1,256,1024]{2,1,0:T(8,128)(2,1)} collective-permute-done((bf16[1,256,1024]{2,1,0:T(8,128)(2,1)S(1)}, bf16[1,256,1024]{2,1,0:T(8,128)(2,1)}, u32[]{:S(2)}, u32[]{:S(2)}) %collective-permute-start.11) | collective-permute-done | bytes 524320 | tf_op jit(solution)/shard_map/ppermute | solution.py:224
  68.3 3.9 %collective-permute-start.8 = (bf16[2,256,1024]{2,1,0:T(8,128)(2,1)S(1)}, bf16[2,256,1024]{2,1,0:T(8,128)(2,1)S(1)}, u32[]{:S(2)}, u32[]{:S(2)}) collective-permute-start(bf16[2,256,1024]{2,1,0:T(8,128)(2,1)S(1)} %collective-permute-done.3.rest_1_), channel_id=1, source_target_pairs={{0,16},{16,0},{32,48},{48,32},{64,80},{80,64},{96,112},{112,96},{1... | collective-permute-start | bytes 3145736 | tf_op jit(solution)/shard_map/ppermute | solution.py:224
  72.7 9.5 %collective-permute-done.12.rest_10_ = bf16[1,256,1024]{2,1,0:T(8,128)(2,1)} collective-permute-done((bf16[1,256,1024]{2,1,0:T(8,128)(2,1)}, bf16[1,256,1024]{2,1,0:T(8,128)(2,1)}, u32[]{:S(2)}, u32[]{:S(2)}) %collective-permute-start.12) | collective-permute-done | bytes 524320 | tf_op jit(solution)/shard_map/ppermute | solution.py:224
  82.8 1.0 copy-done.7
  84.8 1.3 %collective-permute-done.15.rest_11_ = bf16[1,256,1024]{2,1,0:T(8,128)(2,1)} collective-permute-done((bf16[1,256,1024]{2,1,0:T(8,128)(2,1)}, bf16[1,256,1024]{2,1,0:T(8,128)(2,1)}, u32[]{:S(2)}, u32[]{:S(2)}) %collective-permute-start.15) | collective-permute-done | bytes 524320 | tf_op jit(solution)/shard_map/ppermute | solution.py:224
  87.5 19.3 %shard_map.104 = (bf16[128,8192]{1,0:T(8,128)(2,1)}, bf16[128,12288]{1,0:T(8,128)(2,1)}, bf16[128,576]{1,0:T(8,128)(2,1)}, bf16[128,576]{1,0:T(8,128)(2,1)}) custom-call(s32[14]{0:T(128)} %concatenate.21.order_ref, bf16[256,768]{1,0:T(8,128)(2,1)} %fusion.3.rows_hbm, ...), custom_call_target="tpu_custom_call", output_to_operand_aliasing={{0}: (18, {}), {1}: (19, {})} | custom-call | flops 40000000000 | bytes 18000000 | tf_op jit(solution)/shard_map/pallas_call | solution.py:169
  106.8 4.1 %all-to-all-start.1 = ((bf16[16,8,576]{2,1,0:T(8,128)(2,1)}), bf16[16,8,576]{2,1,0:T(8,128)(2,1)S(1)}, u32[]{:S(2)}, u32[]{:S(2)}) async-start(bf16[16,8,576]{2,1,0:T(8,128)(2,1)} %bitcast.38), calls=%async_computation.1 | async-start | bytes 327680 | tf_op jit(solution)/shard_map/all_to_all | solution.py:312
  111.0 1.9 %reshape.41 = bf16[1,73728]{1,0:T(2,128)(2,1)} reshape(bf16[128,576]{1,0:T(8,128)(2,1)} %get-tuple-element.45) | data formatting | bytes 294912 | tf_op jit(solution)/shard_map/reshape | solution.py:314
  112.9 5.0 %all-to-all-done.1 = bf16[16,8,576]{2,1,0:T(8,128)(2,1)S(1)} async-done(((bf16[16,8,576]{2,1,0:T(8,128)(2,1)}), bf16[16,8,576]{2,1,0:T(8,128)(2,1)S(1)}, u32[]{:S(2)}, u32[]{:S(2)}) %all-to-all-start.1) | async-done | bytes 147488 | tf_op jit(solution)/shard_map/all_to_all | solution.py:312
  (57 shorter events, 9.6 us)
Async XLA Ops:
  0.6 18.2 %copy-start.4 = (s32[1,128]{1,0:T(1,128)S(1)}, s32[1,128]{1,0:T(1,128)}, u32[]{:S(2)}) copy-start(s32[1,128]{1,0:T(1,128)} %param.12) | copy-start | bytes 1540
  0.7 18.3 %copy-start = (bf16[1,73728]{1,0:T(2,128)(2,1)S(1)}, bf16[1,73728]{1,0:T(2,128)(2,1)}, u32[]{:S(2)}) copy-start(bf16[1,73728]{1,0:T(2,128)(2,1)} %param.8) | copy-start | bytes 442372
  0.7 5.8 %collective-permute-start = (bf16[512,1024]{1,0:T(8,128)(2,1)}, bf16[512,1024]{1,0:T(8,128)(2,1)S(1)}, u32[]{:S(2)}, u32[]{:S(2)}) collective-permute-start(bf16[512,1024]{1,0:T(8,128)(2,1)} %param.11), channel_id=1, source_target_pairs={{0,16},{16,0},{32,48},{48,32},{64,80},{80,64},{96,112},{112,96},{1... | collective-permute-start | bytes 3145736 | tf_op jit(solution)/shard_map/ppermute | solution.py:224
  6.5 22.1 %copy-start.2 = (bf16[512,1024]{1,0:T(8,128)(2,1)}, bf16[512,1024]{1,0:T(8,128)(2,1)S(1)}, u32[]{:S(2)}) copy-start(bf16[512,1024]{1,0:T(8,128)(2,1)S(1)} %collective-permute-done) | copy-start | bytes 3145732
  6.6 19.8 %collective-permute-start.1 = (bf16[2,256,1024]{2,1,0:T(8,128)(2,1)S(1)}, bf16[2,256,1024]{2,1,0:T(8,128)(2,1)}, u32[]{:S(2)}, u32[]{:S(2)}) collective-permute-start(bf16[2,256,1024]{2,1,0:T(8,128)(2,1)S(1)} %pad_maximum_fusion), channel_id=1, source_target_pairs={{0,32},{32,64},{64,96},{96,128},{128,160},{160,192},{192,224},{224... | collective-permute-start | bytes 3145736 | tf_op jit(solution)/shard_map/ppermute | solution.py:224
  12.1 13.6 %all-to-all-start = ((bf16[16,8,576]{2,1,0:T(8,128)(2,1)}), bf16[16,8,576]{2,1,0:T(8,128)(2,1)S(1)}, u32[]{:S(2)}, u32[]{:S(2)}) async-start(bf16[16,8,576]{2,1,0:T(8,128)(2,1)} %tile.9), calls=%async_computation | async-start | bytes 327680 | tf_op jit(solution)/shard_map/all_to_all | solution.py:261
  26.5 14.3 %collective-permute-start.3 = (bf16[2,256,1024]{2,1,0:T(8,128)(2,1)}, bf16[2,256,1024]{2,1,0:T(8,128)(2,1)S(1)}, u32[]{:S(2)}, u32[]{:S(2)}) collective-permute-start(bf16[2,256,1024]{2,1,0:T(8,128)(2,1)} %collective-permute-done.1.rest_1_), channel_id=1, source_target_pairs={{0,32},{32,64},{64,96},{96,128},{128,160},{160,192},{192,224},{224... | collective-permute-start | bytes 3145736 | tf_op jit(solution)/shard_map/ppermute | solution.py:224
  27.8 15.2 %collective-permute-start.2 = (bf16[2,256,1024]{2,1,0:T(8,128)(2,1)}, bf16[2,256,1024]{2,1,0:T(8,128)(2,1)}, u32[]{:S(2)}, u32[]{:S(2)}) collective-permute-start(bf16[2,256,1024]{2,1,0:T(8,128)(2,1)} %collective-permute-done.1.rest_1_), channel_id=1, source_target_pairs={{0,4},{32,36},{64,68},{96,100},{128,132},{160,164},{192,196},{224,... | collective-permute-start | bytes 3145736 | tf_op jit(solution)/shard_map/ppermute | solution.py:224
  28.6 17.5 %collective-permute-start.5 = (bf16[2,256,1024]{2,1,0:T(8,128)(2,1)}, bf16[2,256,1024]{2,1,0:T(8,128)(2,1)}, u32[]{:S(2)}, u32[]{:S(2)}) collective-permute-start(bf16[2,256,1024]{2,1,0:T(8,128)(2,1)} %collective-permute-done.1.rest_1_), channel_id=1, source_target_pairs={{0,16},{16,0},{32,48},{48,32},{64,80},{80,64},{96,112},{112,96},{1... | collective-permute-start | bytes 3145736 | tf_op jit(solution)/shard_map/ppermute | solution.py:224
  40.7 27.6 %copy-start.5 = (bf16[2,256,1024]{2,1,0:T(8,128)(2,1)}, bf16[2,256,1024]{2,1,0:T(8,128)(2,1)S(1)}, u32[]{:S(2)}) copy-start(bf16[2,256,1024]{2,1,0:T(8,128)(2,1)S(1)} %collective-permute-done.3.rest_1_) | copy-start | bytes 3145732
  43.0 3.1 %collective-permute-start.6 = (bf16[2,256,1024]{2,1,0:T(8,128)(2,1)}, bf16[2,256,1024]{2,1,0:T(8,128)(2,1)}, u32[]{:S(2)}, u32[]{:S(2)}) collective-permute-start(bf16[2,256,1024]{2,1,0:T(8,128)(2,1)} %collective-permute-done.2.rest_2_), channel_id=1, source_target_pairs={{0,16},{16,0},{32,48},{48,32},{64,80},{80,64},{96,112},{112,96},{1... | collective-permute-start | bytes 3145736 | tf_op jit(solution)/shard_map/ppermute | solution.py:224
  43.7 28.5 %collective-permute-start.7 = (bf16[2,256,1024]{2,1,0:T(8,128)(2,1)S(1)}, bf16[2,256,1024]{2,1,0:T(8,128)(2,1)S(1)}, u32[]{:S(2)}, u32[]{:S(2)}) collective-permute-start(bf16[2,256,1024]{2,1,0:T(8,128)(2,1)S(1)} %collective-permute-done.3.rest_1_), channel_id=1, source_target_pairs={{0,4},{32,36},{64,68},{96,100},{128,132},{160,164},{192,196},{224,... | collective-permute-start | bytes 3145736 | tf_op jit(solution)/shard_map/ppermute | solution.py:224
  43.7 14.1 %collective-permute-start.4 = (bf16[2,256,1024]{2,1,0:T(8,128)(2,1)S(1)}, bf16[2,256,1024]{2,1,0:T(8,128)(2,1)S(1)}, u32[]{:S(2)}, u32[]{:S(2)}) collective-permute-start(bf16[2,256,1024]{2,1,0:T(8,128)(2,1)S(1)} %collective-permute-done.3.rest_1_), channel_id=1, source_target_pairs={{0,32},{32,64},{64,96},{96,128},{128,160},{160,192},{192,224},{224... | collective-permute-start | bytes 3145736 | tf_op jit(solution)/shard_map/ppermute | solution.py:224
  57.8 28.9 %copy-start.1 = (bf16[2,256,1024]{2,1,0:T(8,128)(2,1)}, bf16[2,256,1024]{2,1,0:T(8,128)(2,1)S(1)}, u32[]{:S(2)}) copy-start(bf16[2,256,1024]{2,1,0:T(8,128)(2,1)S(1)} %collective-permute-done.4.rest_5_) | copy-start | bytes 3145732
  57.9 9.9 %collective-permute-start.11 = (bf16[1,256,1024]{2,1,0:T(8,128)(2,1)S(1)}, bf16[1,256,1024]{2,1,0:T(8,128)(2,1)}, u32[]{:S(2)}, u32[]{:S(2)}) collective-permute-start(bf16[1,256,1024]{2,1,0:T(8,128)(2,1)S(1)} %slice.7), channel_id=1, source_target_pairs={{0,32},{32,64},{64,96},{96,128},{128,160},{160,192},{192,224},{224... | collective-permute-start | bytes 1572872 | tf_op jit(solution)/shard_map/ppermute | solution.py:224
  61.3 20.9 %collective-permute-start.10 = (bf16[2,256,1024]{2,1,0:T(8,128)(2,1)S(1)}, bf16[2,256,1024]{2,1,0:T(8,128)(2,1)}, u32[]{:S(2)}, u32[]{:S(2)}) collective-permute-start(bf16[2,256,1024]{2,1,0:T(8,128)(2,1)S(1)} %collective-permute-done.4.rest_5_), channel_id=1, source_target_pairs={{0,4},{32,36},{64,68},{96,100},{128,132},{160,164},{192,196},{224,... | collective-permute-start | bytes 3145736 | tf_op jit(solution)/shard_map/ppermute | solution.py:224
  67.8 14.4 %collective-permute-start.12 = (bf16[1,256,1024]{2,1,0:T(8,128)(2,1)}, bf16[1,256,1024]{2,1,0:T(8,128)(2,1)}, u32[]{:S(2)}, u32[]{:S(2)}) collective-permute-start(bf16[1,256,1024]{2,1,0:T(8,128)(2,1)} %collective-permute-done.11.rest_9_), channel_id=1, source_target_pairs={{0,4},{32,36},{64,68},{96,100},{128,132},{160,164},{192,196},{224,... | collective-permute-start | bytes 1572872 | tf_op jit(solution)/shard_map/ppermute | solution.py:224
  68.3 14.5 %collective-permute-start.8 = (bf16[2,256,1024]{2,1,0:T(8,128)(2,1)S(1)}, bf16[2,256,1024]{2,1,0:T(8,128)(2,1)S(1)}, u32[]{:S(2)}, u32[]{:S(2)}) collective-permute-start(bf16[2,256,1024]{2,1,0:T(8,128)(2,1)S(1)} %collective-permute-done.3.rest_1_), channel_id=1, source_target_pairs={{0,16},{16,0},{32,48},{48,32},{64,80},{80,64},{96,112},{112,96},{1... | collective-permute-start | bytes 3145736 | tf_op jit(solution)/shard_map/ppermute | solution.py:224
  72.1 14.0 %collective-permute-start.13 = (bf16[2,256,1024]{2,1,0:T(8,128)(2,1)S(1)}, bf16[2,256,1024]{2,1,0:T(8,128)(2,1)}, u32[]{:S(2)}, u32[]{:S(2)}) collective-permute-start(bf16[2,256,1024]{2,1,0:T(8,128)(2,1)S(1)} %collective-permute-done.4.rest_5_), channel_id=1, source_target_pairs={{0,16},{16,0},{32,48},{48,32},{64,80},{80,64},{96,112},{112,96},{1... | collective-permute-start | bytes 3145736 | tf_op jit(solution)/shard_map/ppermute | solution.py:224
  72.2 14.0 %collective-permute-start.9 = (bf16[2,256,1024]{2,1,0:T(8,128)(2,1)S(1)}, bf16[2,256,1024]{2,1,0:T(8,128)(2,1)}, u32[]{:S(2)}, u32[]{:S(2)}) collective-permute-start(bf16[2,256,1024]{2,1,0:T(8,128)(2,1)S(1)} %collective-permute-done.7.rest_2_), channel_id=1, source_target_pairs={{0,16},{16,0},{32,48},{48,32},{64,80},{80,64},{96,112},{112,96},{1... | collective-permute-start | bytes 3145736 | tf_op jit(solution)/shard_map/ppermute | solution.py:224
  82.2 4.6 %collective-permute-start.14 = (bf16[2,256,1024]{2,1,0:T(8,128)(2,1)}, bf16[2,256,1024]{2,1,0:T(8,128)(2,1)}, u32[]{:S(2)}, u32[]{:S(2)}) collective-permute-start(bf16[2,256,1024]{2,1,0:T(8,128)(2,1)} %collective-permute-done.10.rest_6_), channel_id=1, source_target_pairs={{0,16},{16,0},{32,48},{48,32},{64,80},{80,64},{96,112},{112,96},{1... | collective-permute-start | bytes 3145736 | tf_op jit(solution)/shard_map/ppermute | solution.py:224
  82.8 3.4 %collective-permute-start.15 = (bf16[1,256,1024]{2,1,0:T(8,128)(2,1)}, bf16[1,256,1024]{2,1,0:T(8,128)(2,1)}, u32[]{:S(2)}, u32[]{:S(2)}) collective-permute-start(bf16[1,256,1024]{2,1,0:T(8,128)(2,1)} %collective-permute-done.11.rest_9_), channel_id=1, source_target_pairs={{0,16},{16,0},{32,48},{48,32},{64,80},{80,64},{96,112},{112,96},{1... | collective-permute-start | bytes 1572872 | tf_op jit(solution)/shard_map/ppermute | solution.py:224
  83.8 3.0 %collective-permute-start.16 = (bf16[1,256,1024]{2,1,0:T(8,128)(2,1)}, bf16[1,256,1024]{2,1,0:T(8,128)(2,1)S(1)}, u32[]{:S(2)}, u32[]{:S(2)}) collective-permute-start(bf16[1,256,1024]{2,1,0:T(8,128)(2,1)} %collective-permute-done.12.rest_10_), channel_id=1, source_target_pairs={{0,16},{16,0},{32,48},{48,32},{64,80},{80,64},{96,112},{112,96},{1... | collective-permute-start | bytes 1572872 | tf_op jit(solution)/shard_map/ppermute | solution.py:224
  106.8 11.0 %all-to-all-start.1 = ((bf16[16,8,576]{2,1,0:T(8,128)(2,1)}), bf16[16,8,576]{2,1,0:T(8,128)(2,1)S(1)}, u32[]{:S(2)}, u32[]{:S(2)}) async-start(bf16[16,8,576]{2,1,0:T(8,128)(2,1)} %bitcast.38), calls=%async_computation.1 | async-start | bytes 327680 | tf_op jit(solution)/shard_map/all_to_all | solution.py:312
  (4 other events, 27.0 us)

commit v4 on v2

--- a/solution.py
+++ b/solution.py
@@ -64,21 +64,21 @@
         rows_copy.start()
         ask(0)
         mask_copy.start()
-        ask(1)
         acc_ref[...] = jnp.zeros_like(acc_ref)
         rows_copy.wait()
         mask_copy.wait()
 
-    @pl.when(step == 1)
+    pltpu.make_async_copy(w_all.at[step], w_all.at[step], arrived.at[step]).wait()
+    pltpu.make_async_copy(q_all.at[step], q_all.at[step], loaded.at[step]).wait()
+    pltpu.make_async_copy(g_all.at[step], g_all.at[step], loaded.at[steps + step]).wait()
+
+    @pl.when(step == 0)
     def _():
-        for slot in range(2, steps):
+        for slot in range(1, steps):
             ask(slot)
         if more:
             before_copy.start()
 
-    pltpu.make_async_copy(w_all.at[step], w_all.at[step], arrived.at[step]).wait()
-    pltpu.make_async_copy(q_all.at[step], q_all.at[step], loaded.at[step]).wait()
-    pltpu.make_async_copy(g_all.at[step], g_all.at[step], loaded.at[steps + step]).wait()
     q_ref, g_ref = q_all.at[step], g_all.at[step]
     w = w_all[step]
     kv_ref[...] = mm(rows_ref[:, :DC], w, 1, 0).astype(BF16)

time: 117 us -> 117 us (level)
  no operation moved by 1% of the time
where the time goes in v4:
time: 117 us; the launch traced here: 116 us
  waiting for transfers between devices  40.5 us (35%)
  Pallas kernels  32.2 us (28%)
  starting transfers between devices  31.3 us (27%)
  local copies, waits for them, and re-layouts  8.21 us (7%)
  other arithmetic  2.64 us (2%)
  between operations  1.49 us (1%)
    pallas_call x2, Pallas kernels, attend(): pl.pallas_call(functools.partial(attend_kernel, layout, int(bool(before))...  32.2 us
    ppermute x17, waiting for transfers between devices, send(): return lax.ppermute(a, ('prompt', 'sample'), pairs)  30.6 us
    ppermute x17, starting transfers between devices, send(): return lax.ppermute(a, ('prompt', 'sample'), pairs)  20.1 us
    all_to_all x1, starting transfers between devices, body(): lax.all_to_all(jnp.tile(after(prompt_latent, here).reshape(-1, DL), (16,...  6.75 us
    all_to_all x1, waiting for transfers between devices, body(): lax.all_to_all(prompt_term, 'sample', 0, 0, tiled=True).reshape(16, -1, DL)  4.97 us
    all_to_all x1, waiting for transfers between devices, body(): lax.all_to_all(jnp.tile(after(prompt_latent, here).reshape(-1, DL), (16,...  4.91 us
    all_to_all x1, starting transfers between devices, body(): lax.all_to_all(prompt_term, 'sample', 0, 0, tiled=True).reshape(16, -1, DL)  4.46 us
  transfers between devices with their start and end apart: 19, of which 8 were waited for; matrix products, arithmetic and copies ran while one was open for 7% of the time, Pallas kernels for 11%

profile of v4, /device:TPU:1, one launch (start us, length us, event | category | flops | bytes accessed | tf_op | source)
XLA Modules:
  0.0 116.3 jit_solution(15281006055334380843)
XLA Ops:
  0.7 3.3 %collective-permute-start = (bf16[512,1024]{1,0:T(8,128)(2,1)}, bf16[512,1024]{1,0:T(8,128)(2,1)S(1)}, u32[]{:S(2)}, u32[]{:S(2)}) collective-permute-start(bf16[512,1024]{1,0:T(8,128)(2,1)} %param.11), channel_id=1, source_target_pairs={{0,16},{16,0},{32,48},{48,32},{64,80},{80,64},{96,112},{112,96},{1... | collective-permute-start | bytes 3145736 | tf_op jit(solution)/shard_map/ppermute | solution.py:224
  4.0 1.1 dynamic-slice_bitcast_fusion.1
  5.1 1.4 %collective-permute-done = bf16[512,1024]{1,0:T(8,128)(2,1)S(1)} collective-permute-done((bf16[512,1024]{1,0:T(8,128)(2,1)}, bf16[512,1024]{1,0:T(8,128)(2,1)S(1)}, u32[]{:S(2)}, u32[]{:S(2)}) %collective-permute-start) | collective-permute-done | bytes 1048608 | tf_op jit(solution)/shard_map/ppermute | solution.py:224
  6.6 3.9 %collective-permute-start.1 = (bf16[2,256,1024]{2,1,0:T(8,128)(2,1)S(1)}, bf16[2,256,1024]{2,1,0:T(8,128)(2,1)}, u32[]{:S(2)}, u32[]{:S(2)}) collective-permute-start(bf16[2,256,1024]{2,1,0:T(8,128)(2,1)S(1)} %pad_maximum_fusion), channel_id=1, source_target_pairs={{0,32},{32,64},{64,96},{96,128},{128,160},{160,192},{192,224},{224... | collective-permute-start | bytes 3145736 | tf_op jit(solution)/shard_map/ppermute | solution.py:224
  12.1 6.8 %all-to-all-start = ((bf16[16,8,576]{2,1,0:T(8,128)(2,1)}), bf16[16,8,576]{2,1,0:T(8,128)(2,1)S(1)}, u32[]{:S(2)}, u32[]{:S(2)}) async-start(bf16[16,8,576]{2,1,0:T(8,128)(2,1)} %tile.9), calls=%async_computation | async-start | bytes 327680 | tf_op jit(solution)/shard_map/all_to_all | solution.py:262
  20.7 4.9 %all-to-all-done = bf16[16,8,576]{2,1,0:T(8,128)(2,1)S(1)} async-done(((bf16[16,8,576]{2,1,0:T(8,128)(2,1)}), bf16[16,8,576]{2,1,0:T(8,128)(2,1)S(1)}, u32[]{:S(2)}, u32[]{:S(2)}) %all-to-all-start) | async-done | bytes 147488 | tf_op jit(solution)/shard_map/all_to_all | solution.py:262
  26.6 1.2 %collective-permute-start.2 = (bf16[2,256,1024]{2,1,0:T(8,128)(2,1)}, bf16[2,256,1024]{2,1,0:T(8,128)(2,1)S(1)}, u32[]{:S(2)}, u32[]{:S(2)}) collective-permute-start(bf16[2,256,1024]{2,1,0:T(8,128)(2,1)} %collective-permute-done.1.rest_2_), channel_id=1, source_target_pairs={{0,32},{32,64},{64,96},{96,128},{128,160},{160,192},{192,224},{224... | collective-permute-start | bytes 3145736 | tf_op jit(solution)/shard_map/ppermute | solution.py:224
  27.9 13.9 %collective-permute-done.4.rest_3_ = bf16[2,256,1024]{2,1,0:T(8,128)(2,1)} collective-permute-done((bf16[2,256,1024]{2,1,0:T(8,128)(2,1)}, bf16[2,256,1024]{2,1,0:T(8,128)(2,1)}, u32[]{:S(2)}, u32[]{:S(2)}) %collective-permute-start.4) | collective-permute-done | bytes 1048608 | tf_op jit(solution)/shard_map/ppermute | solution.py:224
  42.5 3.5 %collective-permute-start.3 = (bf16[2,256,1024]{2,1,0:T(8,128)(2,1)S(1)}, bf16[2,256,1024]{2,1,0:T(8,128)(2,1)S(1)}, u32[]{:S(2)}, u32[]{:S(2)}) collective-permute-start(bf16[2,256,1024]{2,1,0:T(8,128)(2,1)S(1)} %collective-permute-done.2.rest_1_), channel_id=1, source_target_pairs={{0,32},{32,64},{64,96},{96,128},{128,160},{160,192},{192,224},{224... | collective-permute-start | bytes 3145736 | tf_op jit(solution)/shard_map/ppermute | solution.py:224
  46.1 12.9 %shard_map.102 = (bf16[128,8192]{1,0:T(8,128)(2,1)}, bf16[128,12288]{1,0:T(8,128)(2,1)}, f32[256,768]{1,0:T(8,128)}) custom-call(s32[10]{0:T(128)} %concatenate.21.order_ref, bf16[256,768]{1,0:T(8,128)(2,1)} %fusion.3.rows_hbm, f32[136,128]{1,0:T(8,128)} %pad_maximum_fusion.1.mask_hbm, bf16[128,12288]{1,0:T(8,128)(2,1)} %bitcast.40, ...), custom_call_target="tpu_custom_call" | custom-call | flops 24000000000 | bytes 10800000 | tf_op jit(solution)/shard_map/pallas_call | solution.py:169
  59.7 0.9 collective-permute-start.8
  60.7 1.2 %collective-permute-start.13 = (bf16[1,256,1024]{2,1,0:T(8,128)(2,1)S(1)}, bf16[1,256,1024]{2,1,0:T(8,128)(2,1)}, u32[]{:S(2)}, u32[]{:S(2)}) collective-permute-start(bf16[1,256,1024]{2,1,0:T(8,128)(2,1)S(1)} %slice.7), channel_id=1, source_target_pairs={{0,32},{32,64},{64,96},{96,128},{128,160},{160,192},{192,224},{224... | collective-permute-start | bytes 1572872 | tf_op jit(solution)/shard_map/ppermute | solution.py:224
  62.4 6.7 %collective-permute-done.13.rest_9_ = bf16[1,256,1024]{2,1,0:T(8,128)(2,1)} collective-permute-done((bf16[1,256,1024]{2,1,0:T(8,128)(2,1)S(1)}, bf16[1,256,1024]{2,1,0:T(8,128)(2,1)}, u32[]{:S(2)}, u32[]{:S(2)}) %collective-permute-start.13) | collective-permute-done | bytes 524320 | tf_op jit(solution)/shard_map/ppermute | solution.py:224
  69.2 1.2 %collective-permute-start.14 = (bf16[1,256,1024]{2,1,0:T(8,128)(2,1)}, bf16[1,256,1024]{2,1,0:T(8,128)(2,1)}, u32[]{:S(2)}, u32[]{:S(2)}) collective-permute-start(bf16[1,256,1024]{2,1,0:T(8,128)(2,1)} %collective-permute-done.13.rest_9_), channel_id=1, source_target_pairs={{0,4},{32,36},{64,68},{96,100},{128,132},{160,164},{192,196},{224,... | collective-permute-start | bytes 1572872 | tf_op jit(solution)/shard_map/ppermute | solution.py:224
  70.4 4.0 %collective-permute-done.10.rest_6_ = bf16[2,256,1024]{2,1,0:T(8,128)(2,1)} collective-permute-done((bf16[2,256,1024]{2,1,0:T(8,128)(2,1)S(1)}, bf16[2,256,1024]{2,1,0:T(8,128)(2,1)}, u32[]{:S(2)}, u32[]{:S(2)}) %collective-permute-start.10) | collective-permute-done | bytes 1048608 | tf_op jit(solution)/shard_map/ppermute | solution.py:224
  74.3 1.3 %collective-permute-start.12 = (bf16[2,256,1024]{2,1,0:T(8,128)(2,1)}, bf16[2,256,1024]{2,1,0:T(8,128)(2,1)S(1)}, u32[]{:S(2)}, u32[]{:S(2)}) collective-permute-start(bf16[2,256,1024]{2,1,0:T(8,128)(2,1)} %collective-permute-done.10.rest_6_), channel_id=1, source_target_pairs={{0,16},{16,0},{32,48},{48,32},{64,80},{80,64},{96,112},{112,96},{1... | collective-permute-start | bytes 3145736 | tf_op jit(solution)/shard_map/ppermute | solution.py:224
  75.6 1.0 copy-done.6
  76.6 3.3 %collective-permute-done.14.rest_10_ = bf16[1,256,1024]{2,1,0:T(8,128)(2,1)} collective-permute-done((bf16[1,256,1024]{2,1,0:T(8,128)(2,1)}, bf16[1,256,1024]{2,1,0:T(8,128)(2,1)}, u32[]{:S(2)}, u32[]{:S(2)}) %collective-permute-start.14) | collective-permute-done | bytes 524320 | tf_op jit(solution)/shard_map/ppermute | solution.py:224
  79.9 2.0 %collective-permute-start.16 = (bf16[1,256,1024]{2,1,0:T(8,128)(2,1)}, bf16[1,256,1024]{2,1,0:T(8,128)(2,1)S(1)}, u32[]{:S(2)}, u32[]{:S(2)}) collective-permute-start(bf16[1,256,1024]{2,1,0:T(8,128)(2,1)} %collective-permute-done.14.rest_10_), channel_id=1, source_target_pairs={{0,16},{16,0},{32,48},{48,32},{64,80},{80,64},{96,112},{112,96},{1... | collective-permute-start | bytes 1572872 | tf_op jit(solution)/shard_map/ppermute | solution.py:224
  82.5 1.1 collective-permute-done.16.rest_12_
  84.9 19.3 %shard_map.103 = (bf16[128,8192]{1,0:T(8,128)(2,1)}, bf16[128,12288]{1,0:T(8,128)(2,1)}, bf16[128,576]{1,0:T(8,128)(2,1)}, bf16[128,576]{1,0:T(8,128)(2,1)}) custom-call(s32[14]{0:T(128)} %concatenate.17.order_ref, bf16[256,768]{1,0:T(8,128)(2,1)} %fusion.3.rows_hbm, ...), custom_call_target="tpu_custom_call", output_to_operand_aliasing={{0}: (18, {}), {1}: (19, {})} | custom-call | flops 40000000000 | bytes 18000000 | tf_op jit(solution)/shard_map/pallas_call | solution.py:169
  104.2 4.5 %all-to-all-start.1 = ((bf16[16,8,576]{2,1,0:T(8,128)(2,1)}), bf16[16,8,576]{2,1,0:T(8,128)(2,1)S(1)}, u32[]{:S(2)}, u32[]{:S(2)}) async-start(bf16[16,8,576]{2,1,0:T(8,128)(2,1)} %bitcast.38), calls=%async_computation.1 | async-start | bytes 327680 | tf_op jit(solution)/shard_map/all_to_all | solution.py:305
  108.7 1.9 %reshape.41 = bf16[1,73728]{1,0:T(2,128)(2,1)} reshape(bf16[128,576]{1,0:T(8,128)(2,1)} %get-tuple-element.29) | data formatting | bytes 294912 | tf_op jit(solution)/shard_map/reshape | solution.py:307
  110.5 5.0 %all-to-all-done.1 = bf16[16,8,576]{2,1,0:T(8,128)(2,1)S(1)} async-done(((bf16[16,8,576]{2,1,0:T(8,128)(2,1)}), bf16[16,8,576]{2,1,0:T(8,128)(2,1)S(1)}, u32[]{:S(2)}, u32[]{:S(2)}) %all-to-all-start.1) | async-done | bytes 147488 | tf_op jit(solution)/shard_map/all_to_all | solution.py:305
  (57 shorter events, 8.4 us)
Async XLA Ops:
  0.6 18.2 %copy-start.4 = (s32[1,128]{1,0:T(1,128)S(1)}, s32[1,128]{1,0:T(1,128)}, u32[]{:S(2)}) copy-start(s32[1,128]{1,0:T(1,128)} %param.12) | copy-start | bytes 1540
  0.7 18.3 %copy-start = (bf16[1,73728]{1,0:T(2,128)(2,1)S(1)}, bf16[1,73728]{1,0:T(2,128)(2,1)}, u32[]{:S(2)}) copy-start(bf16[1,73728]{1,0:T(2,128)(2,1)} %param.8) | copy-start | bytes 442372
  0.7 5.8 %collective-permute-start = (bf16[512,1024]{1,0:T(8,128)(2,1)}, bf16[512,1024]{1,0:T(8,128)(2,1)S(1)}, u32[]{:S(2)}, u32[]{:S(2)}) collective-permute-start(bf16[512,1024]{1,0:T(8,128)(2,1)} %param.11), channel_id=1, source_target_pairs={{0,16},{16,0},{32,48},{48,32},{64,80},{80,64},{96,112},{112,96},{1... | collective-permute-start | bytes 3145736 | tf_op jit(solution)/shard_map/ppermute | solution.py:224
  6.5 39.6 %copy-start.2 = (bf16[512,1024]{1,0:T(8,128)(2,1)}, bf16[512,1024]{1,0:T(8,128)(2,1)S(1)}, u32[]{:S(2)}) copy-start(bf16[512,1024]{1,0:T(8,128)(2,1)S(1)} %collective-permute-done) | copy-start | bytes 3145732
  6.6 19.8 %collective-permute-start.1 = (bf16[2,256,1024]{2,1,0:T(8,128)(2,1)S(1)}, bf16[2,256,1024]{2,1,0:T(8,128)(2,1)}, u32[]{:S(2)}, u32[]{:S(2)}) collective-permute-start(bf16[2,256,1024]{2,1,0:T(8,128)(2,1)S(1)} %pad_maximum_fusion), channel_id=1, source_target_pairs={{0,32},{32,64},{64,96},{96,128},{128,160},{160,192},{192,224},{224... | collective-permute-start | bytes 3145736 | tf_op jit(solution)/shard_map/ppermute | solution.py:224
  12.1 13.6 %all-to-all-start = ((bf16[16,8,576]{2,1,0:T(8,128)(2,1)}), bf16[16,8,576]{2,1,0:T(8,128)(2,1)S(1)}, u32[]{:S(2)}, u32[]{:S(2)}) async-start(bf16[16,8,576]{2,1,0:T(8,128)(2,1)} %tile.9), calls=%async_computation | async-start | bytes 327680 | tf_op jit(solution)/shard_map/all_to_all | solution.py:262
  26.5 15.4 %collective-permute-start.4 = (bf16[2,256,1024]{2,1,0:T(8,128)(2,1)}, bf16[2,256,1024]{2,1,0:T(8,128)(2,1)}, u32[]{:S(2)}, u32[]{:S(2)}) collective-permute-start(bf16[2,256,1024]{2,1,0:T(8,128)(2,1)} %collective-permute-done.1.rest_2_), channel_id=1, source_target_pairs={{0,4},{32,36},{64,68},{96,100},{128,132},{160,164},{192,196},{224,... | collective-permute-start | bytes 3145736 | tf_op jit(solution)/shard_map/ppermute | solution.py:224
  26.6 15.9 %collective-permute-start.2 = (bf16[2,256,1024]{2,1,0:T(8,128)(2,1)}, bf16[2,256,1024]{2,1,0:T(8,128)(2,1)S(1)}, u32[]{:S(2)}, u32[]{:S(2)}) collective-permute-start(bf16[2,256,1024]{2,1,0:T(8,128)(2,1)} %collective-permute-done.1.rest_2_), channel_id=1, source_target_pairs={{0,32},{32,64},{64,96},{96,128},{128,160},{160,192},{192,224},{224... | collective-permute-start | bytes 3145736 | tf_op jit(solution)/shard_map/ppermute | solution.py:224
  27.9 18.2 %collective-permute-start.5 = (bf16[2,256,1024]{2,1,0:T(8,128)(2,1)}, bf16[2,256,1024]{2,1,0:T(8,128)(2,1)}, u32[]{:S(2)}, u32[]{:S(2)}) collective-permute-start(bf16[2,256,1024]{2,1,0:T(8,128)(2,1)} %collective-permute-done.1.rest_2_), channel_id=1, source_target_pairs={{0,16},{16,0},{32,48},{48,32},{64,80},{80,64},{96,112},{112,96},{1... | collective-permute-start | bytes 3145736 | tf_op jit(solution)/shard_map/ppermute | solution.py:224
  41.8 4.2 %collective-permute-start.6 = (bf16[2,256,1024]{2,1,0:T(8,128)(2,1)}, bf16[2,256,1024]{2,1,0:T(8,128)(2,1)}, u32[]{:S(2)}, u32[]{:S(2)}) collective-permute-start(bf16[2,256,1024]{2,1,0:T(8,128)(2,1)} %collective-permute-done.4.rest_3_), channel_id=1, source_target_pairs={{0,16},{16,0},{32,48},{48,32},{64,80},{80,64},{96,112},{112,96},{1... | collective-permute-start | bytes 3145736 | tf_op jit(solution)/shard_map/ppermute | solution.py:224
  42.5 17.2 %copy-start.5 = (bf16[2,256,1024]{2,1,0:T(8,128)(2,1)}, bf16[2,256,1024]{2,1,0:T(8,128)(2,1)S(1)}, u32[]{:S(2)}) copy-start(bf16[2,256,1024]{2,1,0:T(8,128)(2,1)S(1)} %collective-permute-done.2.rest_1_) | copy-start | bytes 3145732
  42.5 19.4 %collective-permute-start.7 = (bf16[2,256,1024]{2,1,0:T(8,128)(2,1)S(1)}, bf16[2,256,1024]{2,1,0:T(8,128)(2,1)}, u32[]{:S(2)}, u32[]{:S(2)}) collective-permute-start(bf16[2,256,1024]{2,1,0:T(8,128)(2,1)S(1)} %collective-permute-done.2.rest_1_), channel_id=1, source_target_pairs={{0,4},{32,36},{64,68},{96,100},{128,132},{160,164},{192,196},{224,... | collective-permute-start | bytes 3145736 | tf_op jit(solution)/shard_map/ppermute | solution.py:224
  42.5 16.4 %collective-permute-start.3 = (bf16[2,256,1024]{2,1,0:T(8,128)(2,1)S(1)}, bf16[2,256,1024]{2,1,0:T(8,128)(2,1)S(1)}, u32[]{:S(2)}, u32[]{:S(2)}) collective-permute-start(bf16[2,256,1024]{2,1,0:T(8,128)(2,1)S(1)} %collective-permute-done.2.rest_1_), channel_id=1, source_target_pairs={{0,32},{32,64},{64,96},{96,128},{128,160},{160,192},{192,224},{224... | collective-permute-start | bytes 3145736 | tf_op jit(solution)/shard_map/ppermute | solution.py:224
  59.0 24.7 %copy-start.1 = (bf16[2,256,1024]{2,1,0:T(8,128)(2,1)}, bf16[2,256,1024]{2,1,0:T(8,128)(2,1)S(1)}, u32[]{:S(2)}) copy-start(bf16[2,256,1024]{2,1,0:T(8,128)(2,1)S(1)} %collective-permute-done.3.rest_5_) | copy-start | bytes 3145732
  59.0 15.3 %collective-permute-start.10 = (bf16[2,256,1024]{2,1,0:T(8,128)(2,1)S(1)}, bf16[2,256,1024]{2,1,0:T(8,128)(2,1)}, u32[]{:S(2)}, u32[]{:S(2)}) collective-permute-start(bf16[2,256,1024]{2,1,0:T(8,128)(2,1)S(1)} %collective-permute-done.3.rest_5_), channel_id=1, source_target_pairs={{0,4},{32,36},{64,68},{96,100},{128,132},{160,164},{192,196},{224,... | collective-permute-start | bytes 3145736 | tf_op jit(solution)/shard_map/ppermute | solution.py:224
  59.7 15.9 %collective-permute-start.8 = (bf16[2,256,1024]{2,1,0:T(8,128)(2,1)S(1)}, bf16[2,256,1024]{2,1,0:T(8,128)(2,1)S(1)}, u32[]{:S(2)}, u32[]{:S(2)}) collective-permute-start(bf16[2,256,1024]{2,1,0:T(8,128)(2,1)S(1)} %collective-permute-done.2.rest_1_), channel_id=1, source_target_pairs={{0,16},{16,0},{32,48},{48,32},{64,80},{80,64},{96,112},{112,96},{1... | collective-permute-start | bytes 3145736 | tf_op jit(solution)/shard_map/ppermute | solution.py:224
  60.7 8.5 %collective-permute-start.13 = (bf16[1,256,1024]{2,1,0:T(8,128)(2,1)S(1)}, bf16[1,256,1024]{2,1,0:T(8,128)(2,1)}, u32[]{:S(2)}, u32[]{:S(2)}) collective-permute-start(bf16[1,256,1024]{2,1,0:T(8,128)(2,1)S(1)} %slice.7), channel_id=1, source_target_pairs={{0,32},{32,64},{64,96},{96,128},{128,160},{160,192},{192,224},{224... | collective-permute-start | bytes 1572872 | tf_op jit(solution)/shard_map/ppermute | solution.py:224
  61.9 20.6 %collective-permute-start.11 = (bf16[2,256,1024]{2,1,0:T(8,128)(2,1)S(1)}, bf16[2,256,1024]{2,1,0:T(8,128)(2,1)}, u32[]{:S(2)}, u32[]{:S(2)}) collective-permute-start(bf16[2,256,1024]{2,1,0:T(8,128)(2,1)S(1)} %collective-permute-done.3.rest_5_), channel_id=1, source_target_pairs={{0,16},{16,0},{32,48},{48,32},{64,80},{80,64},{96,112},{112,96},{1... | collective-permute-start | bytes 3145736 | tf_op jit(solution)/shard_map/ppermute | solution.py:224
  61.9 20.6 %collective-permute-start.9 = (bf16[2,256,1024]{2,1,0:T(8,128)(2,1)}, bf16[2,256,1024]{2,1,0:T(8,128)(2,1)}, u32[]{:S(2)}, u32[]{:S(2)}) collective-permute-start(bf16[2,256,1024]{2,1,0:T(8,128)(2,1)} %collective-permute-done.7.rest_2_), channel_id=1, source_target_pairs={{0,16},{16,0},{32,48},{48,32},{64,80},{80,64},{96,112},{112,96},{1... | collective-permute-start | bytes 3145736 | tf_op jit(solution)/shard_map/ppermute | solution.py:224
  69.2 10.8 %collective-permute-start.14 = (bf16[1,256,1024]{2,1,0:T(8,128)(2,1)}, bf16[1,256,1024]{2,1,0:T(8,128)(2,1)}, u32[]{:S(2)}, u32[]{:S(2)}) collective-permute-start(bf16[1,256,1024]{2,1,0:T(8,128)(2,1)} %collective-permute-done.13.rest_9_), channel_id=1, source_target_pairs={{0,4},{32,36},{64,68},{96,100},{128,132},{160,164},{192,196},{224,... | collective-permute-start | bytes 1572872 | tf_op jit(solution)/shard_map/ppermute | solution.py:224
  74.3 9.4 %collective-permute-start.12 = (bf16[2,256,1024]{2,1,0:T(8,128)(2,1)}, bf16[2,256,1024]{2,1,0:T(8,128)(2,1)S(1)}, u32[]{:S(2)}, u32[]{:S(2)}) collective-permute-start(bf16[2,256,1024]{2,1,0:T(8,128)(2,1)} %collective-permute-done.10.rest_6_), channel_id=1, source_target_pairs={{0,16},{16,0},{32,48},{48,32},{64,80},{80,64},{96,112},{112,96},{1... | collective-permute-start | bytes 3145736 | tf_op jit(solution)/shard_map/ppermute | solution.py:224
  76.6 5.9 %collective-permute-start.15 = (bf16[1,256,1024]{2,1,0:T(8,128)(2,1)}, bf16[1,256,1024]{2,1,0:T(8,128)(2,1)S(1)}, u32[]{:S(2)}, u32[]{:S(2)}) collective-permute-start(bf16[1,256,1024]{2,1,0:T(8,128)(2,1)} %collective-permute-done.13.rest_9_), channel_id=1, source_target_pairs={{0,16},{16,0},{32,48},{48,32},{64,80},{80,64},{96,112},{112,96},{1... | collective-permute-start | bytes 1572872 | tf_op jit(solution)/shard_map/ppermute | solution.py:224
  79.9 3.8 %collective-permute-start.16 = (bf16[1,256,1024]{2,1,0:T(8,128)(2,1)}, bf16[1,256,1024]{2,1,0:T(8,128)(2,1)S(1)}, u32[]{:S(2)}, u32[]{:S(2)}) collective-permute-start(bf16[1,256,1024]{2,1,0:T(8,128)(2,1)} %collective-permute-done.14.rest_10_), channel_id=1, source_target_pairs={{0,16},{16,0},{32,48},{48,32},{64,80},{80,64},{96,112},{112,96},{1... | collective-permute-start | bytes 1572872 | tf_op jit(solution)/shard_map/ppermute | solution.py:224
  104.2 11.3 %all-to-all-start.1 = ((bf16[16,8,576]{2,1,0:T(8,128)(2,1)}), bf16[16,8,576]{2,1,0:T(8,128)(2,1)S(1)}, u32[]{:S(2)}, u32[]{:S(2)}) async-start(bf16[16,8,576]{2,1,0:T(8,128)(2,1)} %bitcast.38), calls=%async_computation.1 | async-start | bytes 327680 | tf_op jit(solution)/shard_map/all_to_all | solution.py:305
  (5 other events, 14.8 us)
